TPU v7x, 768 devices: a whole 4x8x12 slice. The times are simulated.
768 devices in a mesh: seq: 16 (over z_lo, x), res: 48 (over z_hi, y, core).
Axes of the slice: x: 4, y: 8, z: 12 (z_hi: 3, z_lo: 4; z = z_hi * 4 + z_lo), core: 2. Of those that a mesh axis runs over, the one named last changes fastest.
Arguments:
- alignment_tensor: float32 [768, 768, 256], P('seq', 'res'), may hold values from -24 to 24
- standardizer_factors: float32 [3, 256], replicated, may hold values from 0.25 to 1.75
- standardizer_offsets: float32 [3, 256], replicated, may hold values from -3 to 3
- horizontal_entry_matrix: bfloat16 [256, 1024], replicated, may hold values from -4 to 4
- horizontal_sigmoid_offset: float32 [256], replicated, may hold values from -4 to 4
- horizontal_exit_matrix: bfloat16 [256, 256], replicated, may hold values from -1 to 1
- horizontal_exit_offset: float32 [256], replicated, may hold values from -2 to 2
- vertical_entry_matrix: bfloat16 [256, 1024], replicated, may hold values from -4 to 4
- vertical_sigmoid_offset: float32 [256], replicated, may hold values from -4 to 4
- vertical_exit_matrix: bfloat16 [256, 256], replicated, may hold values from -1 to 1
- vertical_exit_offset: float32 [256], replicated, may hold values from -2 to 2
- feedforward_first_matrix: bfloat16 [256, 1024], replicated, may hold values from -0.375 to 0.375
- feedforward_first_offset: float32 [1024], replicated, may hold values from -3 to 3
- feedforward_second_matrix: bfloat16 [1024, 256], replicated, may hold values from -0.25 to 0.25
- feedforward_second_offset: float32 [256], replicated, may hold values from -2 to 2
Outputs:
- updated_msa: float32 [768, 768, 256], P('seq', 'res')
All inputs are finite; a program needn't handle non-finite values.
Results may differ from a plain program's by a relative error of at most 0.012.
Values may be sent and summed in bfloat16 or wider, within the bound.
No kernel may reach another device: no remote copies, remote signals or barrier semaphores. Data moves between devices by JAX's collectives and lax.ppermute only.
A program may use at most 32 MiB of HBM per device.

v0:
```python
import jax
import jax.numpy as jnp
from jax import lax
from jax.sharding import PartitionSpec as P

HEADS = 8


def standardize_features(values, gain, shift):
    row_mean = jnp.mean(values, axis=-1, keepdims=True)
    centred = values - row_mean
    variance = jnp.mean(centred * centred, axis=-1, keepdims=True)
    return (centred * lax.rsqrt(variance + 1e-05) * gain + shift).astype(jnp.bfloat16)


def final_mapping(source, weight, offset):
    dims_in = source.shape
    flat = (
        jnp.dot(source.reshape(-1, dims_in[-1]), weight, preferred_element_type=jnp.float32)
        + offset
    )
    return flat.reshape(dims_in[:-1] + (weight.shape[1],))


def attention_core(normed, proj, gate_bias):
    count, length, channels = normed.shape
    head_size = channels // HEADS
    projected = jnp.dot(
        normed.reshape(count * length, channels), proj, preferred_element_type=jnp.float32
    )
    query = (projected[:, :channels] * head_size ** (-0.5)).astype(jnp.bfloat16)
    key_rows = projected[:, channels : 2 * channels].astype(jnp.bfloat16)
    value_rows = projected[:, 2 * channels : 3 * channels].astype(jnp.bfloat16)
    gate_value = jax.nn.sigmoid(projected[:, 3 * channels :] + gate_bias)

    def by_heads(tensor):
        return tensor.reshape(count, length, HEADS, head_size).transpose(2, 0, 1, 3)

    def one_head(triple):
        query_head, key_head, value_head = triple
        scores = jnp.einsum(
            "nqd,nkd->nqk", query_head, key_head, preferred_element_type=jnp.float32
        )
        peak_score = jnp.max(scores, axis=-1, keepdims=True)
        weights = jnp.exp(scores - peak_score)
        row_total = jnp.sum(weights, axis=-1, keepdims=True)
        probabilities = (weights / row_total).astype(jnp.bfloat16)
        return jnp.einsum(
            "nqk,nkd->nqd", probabilities, value_head, preferred_element_type=jnp.float32
        )

    per_head = lax.map(one_head, (by_heads(query), by_heads(key_rows), by_heads(value_rows)))
    merged = per_head.transpose(1, 2, 0, 3).reshape(count * length, channels)
    return (gate_value * merged).astype(jnp.bfloat16).reshape(count, length, channels)


def shards(
    alignment_tensor,
    standardizer_factors,
    standardizer_offsets,
    horizontal_entry_matrix,
    horizontal_sigmoid_offset,
    horizontal_exit_matrix,
    horizontal_exit_offset,
    vertical_entry_matrix,
    vertical_sigmoid_offset,
    vertical_exit_matrix,
    vertical_exit_offset,
    feedforward_first_matrix,
    feedforward_first_offset,
    feedforward_second_matrix,
    feedforward_second_offset,
):
    seq_local, res_local, channels = alignment_tensor.shape
    res_count = lax.axis_size("res")
    seq_count = lax.axis_size("seq")
    standardized_horizontal = standardize_features(
        alignment_tensor, standardizer_factors[0], standardizer_offsets[0]
    )
    row_split = standardized_horizontal.reshape(
        res_count, seq_local // res_count, res_local, channels
    )
    sequences = lax.all_to_all(row_split, "res", split_axis=0, concat_axis=2, tiled=True)
    lead, items, length, width = sequences.shape
    flat_seqs = sequences.reshape(lead * items, length, width)
    horizontal_sigmoid_masked = attention_core(
        flat_seqs, horizontal_entry_matrix, horizontal_sigmoid_offset
    )
    result = final_mapping(
        horizontal_sigmoid_masked, horizontal_exit_matrix, horizontal_exit_offset
    )
    row_remote = result.reshape(lead, items, length, result.shape[-1])
    horizontal_increment = lax.all_to_all(
        row_remote, "res", split_axis=2, concat_axis=0, tiled=True
    ).reshape(seq_local, res_local, channels)
    alignment_horizontal_done = alignment_tensor + horizontal_increment
    standardized_vertical = standardize_features(
        alignment_horizontal_done, standardizer_factors[1], standardizer_offsets[1]
    )
    col_split = standardized_vertical.reshape(
        seq_local, seq_count, res_local // seq_count, channels
    )
    columns = lax.all_to_all(col_split, "seq", split_axis=1, concat_axis=0, tiled=True)
    length, lead, items, width = columns.shape
    turned = columns.reshape(length, lead * items, width).transpose(1, 0, 2)
    vertical_sigmoid_masked = attention_core(turned, vertical_entry_matrix, vertical_sigmoid_offset)
    result = final_mapping(vertical_sigmoid_masked, vertical_exit_matrix, vertical_exit_offset)
    col_remote = result.transpose(1, 0, 2).reshape(length, lead, items, result.shape[-1])
    vertical_increment = (
        lax.all_to_all(
            col_remote.astype(jnp.bfloat16), "seq", split_axis=0, concat_axis=1, tiled=True
        )
        .astype(col_remote.dtype)
        .reshape(seq_local, res_local, channels)
    )
    vertical_done = alignment_horizontal_done + vertical_increment
    normed_trans = standardize_features(
        vertical_done, standardizer_factors[2], standardizer_offsets[2]
    )
    inner = jax.nn.relu(
        final_mapping(normed_trans, feedforward_first_matrix, feedforward_first_offset)
    ).astype(jnp.bfloat16)
    return vertical_done + final_mapping(
        inner, feedforward_second_matrix, feedforward_second_offset
    )


def solution(mesh):
    return jax.shard_map(
        shards,
        mesh=mesh,
        in_specs=(
            P("seq", "res", None),
            P(),
            P(),
            P(),
            P(),
            P(),
            P(),
            P(),
            P(),
            P(),
            P(),
            P(),
            P(),
            P(),
            P(),
        ),
        out_specs=P("seq", "res", None),
        check_vma=False,
    )
```

profile of v0, /device:TPU:16, one launch (start us, length us, event | category | flops | bytes accessed | tf_op | source)
XLA Modules:
  0.0 170.9 jit_solution(9555622059179973236)
XLA Ops:
  0.0 0.8 fusion.58
  0.8 0.8 fusion.59
  1.6 1.3 reduce_sum.72
  2.9 1.4 multiply_reduce_fusion.2
  4.4 2.2 %fusion.45 = bf16[48,1,16,256]{3,2,1,0:T(8,128)(2,1)} fusion(f32[48,16,256]{2,1,0:T(8,128)} %param.19, f32[256]{0:T(256)S(1)} %bitcast.142, f32[256]{0:T(256)S(1)} %bitcast.141, f32[48,16]{1,0:T(8,128)S(1)} %add_rsqrt_fusion.2, f32[48,16]{1,0:T(8,128)S(1)} %broadcast_multiply_fusion.2), kind=kLoop, calls=%fused_computation.63 | loop fusion | flops 983040 | bytes 1187840 | tf_op jit(solution)/shard_map/reshape | solution.py:80
  6.5 19.9 %all-to-all-start = ((bf16[48,1,16,256]{3,2,1,0:T(8,128)(2,1)}), bf16[48,1,16,256]{3,2,1,0:T(8,128)(2,1)S(1)}, u32[]{:S(2)}, u32[]{:S(2)}) async-start(bf16[48,1,16,256]{3,2,1,0:T(8,128)(2,1)} %fusion.45), calls=%async_computation | async-start | bytes 786432 | tf_op jit(solution)/shard_map/all_to_all | solution.py:83
  26.4 18.1 %all-to-all-done = bf16[48,1,16,256]{3,2,1,0:T(8,128)(2,1)S(1)} async-done(((bf16[48,1,16,256]{3,2,1,0:T(8,128)(2,1)}), bf16[48,1,16,256]{3,2,1,0:T(8,128)(2,1)S(1)}, u32[]{:S(2)}, u32[]{:S(2)}) %all-to-all-start) | async-done | bytes 393248 | tf_op jit(solution)/shard_map/all_to_all | solution.py:83
  44.6 2.2 %fusion.60 = (bf16[768,1024]{1,0:T(8,128)(2,1)S(1)}, f32[768,1024]{1,0:T(8,128)}) fusion(bf16[768,256]{1,0:T(8,128)(2,1)S(1)} %bitcast.127, bf16[256,1024]{1,0:T(8,128)(2,1)S(1)} %copy-done), kind=kOutput, calls=%fused_computation.82 | convolution fusion | flops 403439616 | bytes 5636096 | tf_op jit(solution)/shard_map/dot_general | solution.py:28
  47.2 1.2 fusion.37
  48.7 11.3 %while.20 = (s32[]{:T(128)}, f32[8,1,768,32]{2,3,1,0:T(8,128)S(1)}, bf16[8,1,768,32]{2,3,0,1:T(8,128)(2,1)S(1)}, bf16[8,1,768,32]{2,3,0,1:T(8,128)(2,1)S(1)}, bf16[8,1,768,32]{2,3,0,1:T(8,128)(2,1)S(1)}, /*index=5*/s32[]{:T(128)}) while((s32[]{:T(128)}, f32[8,1,768,32]{2,3,1,0:T(8,128)S(1)}, bf16[8,1,768,32]{2,3,0,1:T(8,128)(2,1)S(1)}, ...), condition=%wide.region_5.6_spmd, body=%wide.region_2.5_spmd.sunk | while | flops 79034880 | bytes 7343173 | solution.py:52
  60.4 1.5 fusion.27
  61.9 0.8 copy.125
  62.7 36.8 %all_to_all.42 = f32[1,1,768,256]{3,1,0,2:T(1,128)S(1)} all-to-all(f32[1,1,768,256]{3,1,0,2:T(1,128)S(1)} %copy.125), channel_id=1, replica_groups=mesh['seq'=16,'res'=48] {'res'}, dimensions={2} | all-to-all | bytes 1572864 | tf_op jit(solution)/shard_map/all_to_all | solution.py:93
  100.5 30.3 %all_to_all.43 = bf16[48,16,1,256]{3,0,2,1:T(8,128)(2,1)S(1)} all-to-all(bf16[48,16,1,256]{3,0,2,1:T(8,128)(2,1)S(1)} %copy.126), channel_id=1, replica_groups=mesh['seq'=16,'res'=48] {'seq'}, dimensions={1} | all-to-all | bytes 786432 | tf_op jit(solution)/shard_map/all_to_all | solution.py:103
  130.8 2.2 %fusion.61 = (bf16[768,1024]{1,0:T(8,128)(2,1)S(1)}, f32[768,1024]{1,0:T(8,128)}) fusion(bf16[768,256]{1,0:T(8,128)(2,1)S(1)} %bitcast.128, bf16[256,1024]{1,0:T(8,128)(2,1)S(1)} %copy-done.2), kind=kOutput, calls=%fused_computation.83 | convolution fusion | flops 403439616 | bytes 5636096 | tf_op jit(solution)/shard_map/dot_general | solution.py:28
  133.5 1.2 fusion.31
  135.0 11.3 %while.21 = (s32[]{:T(128)}, f32[8,1,768,32]{2,3,1,0:T(8,128)S(1)}, bf16[8,1,768,32]{2,3,0,1:T(8,128)(2,1)S(1)}, bf16[8,1,768,32]{2,3,0,1:T(8,128)(2,1)S(1)}, bf16[8,1,768,32]{2,3,0,1:T(8,128)(2,1)S(1)}, /*index=5*/s32[]{:T(128)}) while((s32[]{:T(128)}, f32[8,1,768,32]{2,3,1,0:T(8,128)S(1)}, bf16[8,1,768,32]{2,3,0,1:T(8,128)(2,1)S(1)}, ...), condition=%wide.region_11.12_spmd, body=%wide.region_8.11_spmd.sunk | while | flops 79034880 | bytes 7343173 | solution.py:52
  135.0 0.5 fusion.84
  146.6 1.5 fusion.30
  148.6 0.9 reduce.8
  149.6 16.3 %all_to_all.44 = bf16[16,2,6144]{2,1,0:T(2,128)(2,1)S(1)} all-to-all(bf16[16,2,6144]{2,1,0:T(2,128)(2,1)S(1)} %reshape.185), channel_id=1, replica_groups=mesh['seq'=16,'res'=48] {'seq'}, dimensions={0} | all-to-all | bytes 786432 | tf_op jit(solution)/shard_map/all_to_all | solution.py:110
  166.5 0.5 fusion.52
  167.7 2.1 %fusion.28 = f32[768,256]{1,0:T(8,128)S(1)} fusion(bf16[1024,256]{1,0:T(8,128)(2,1)S(1)} %copy-done.3, bf16[768,256]{1,0:T(8,128)(2,1)S(1)} %bitcast.136, bf16[256,1024]{1,0:T(8,128)(2,1)} %param.30, f32[1024]{0:T(1024)S(1)} %copy-done.6, f32[256]{0:T(256)S(1)} %copy-done.11), kind=kOutput, calls=%fused_computation.35 | convolution fusion | flops 807862272 | bytes 2233344 | tf_op jit(solution)/shard_map/dot_general | solution.py:19
  169.8 1.0 add.151
  (101 shorter events, 26.5 us)
Async XLA Ops:
  0.0 44.6 %copy-start = (bf16[256,1024]{1,0:T(8,128)(2,1)S(1)}, bf16[256,1024]{1,0:T(8,128)(2,1)}, u32[]{:S(2)}) copy-start(bf16[256,1024]{1,0:T(8,128)(2,1)} %param.22) | copy-start | bytes 1572868
  6.5 38.0 %all-to-all-start = ((bf16[48,1,16,256]{3,2,1,0:T(8,128)(2,1)}), bf16[48,1,16,256]{3,2,1,0:T(8,128)(2,1)S(1)}, u32[]{:S(2)}, u32[]{:S(2)}) async-start(bf16[48,1,16,256]{3,2,1,0:T(8,128)(2,1)} %fusion.45), calls=%async_computation | async-start | bytes 786432 | tf_op jit(solution)/shard_map/all_to_all | solution.py:83
  48.7 11.6 %copy-start.4 = (bf16[256,256]{1,0:T(8,128)(2,1)S(1)}, bf16[256,256]{1,0:T(8,128)(2,1)}, u32[]{:S(2)}) copy-start(bf16[256,256]{1,0:T(8,128)(2,1)} %param.24) | copy-start | bytes 393220
  48.7 11.6 %copy-start.7 = (f32[256]{0:T(256)S(1)}, f32[256]{0:T(256)}, u32[]{:S(2)}) copy-start(f32[256]{0:T(256)} %param.25) | copy-start | bytes 3076
  48.7 11.6 %copy-start.8 = (f32[256]{0:T(256)S(1)}, f32[256]{0:T(256)}, u32[]{:S(2)}) copy-start(f32[256]{0:T(256)} %param.23) | copy-start | bytes 3076
  61.9 37.7 %copy-start.1 = (f32[48,16,256]{2,1,0:T(8,128)S(1)}, f32[48,16,256]{2,1,0:T(8,128)}, u32[]{:S(2)}) copy-start(f32[48,16,256]{2,1,0:T(8,128)} %param.19) | copy-start | bytes 2359300
  99.8 31.1 %copy-start.2 = (bf16[256,1024]{1,0:T(8,128)(2,1)S(1)}, bf16[256,1024]{1,0:T(8,128)(2,1)}, u32[]{:S(2)}) copy-start(bf16[256,1024]{1,0:T(8,128)(2,1)} %param.26) | copy-start | bytes 1572868
  134.9 11.6 %copy-start.5 = (bf16[256,256]{1,0:T(8,128)(2,1)S(1)}, bf16[256,256]{1,0:T(8,128)(2,1)}, u32[]{:S(2)}) copy-start(bf16[256,256]{1,0:T(8,128)(2,1)} %param.28) | copy-start | bytes 393220
  134.9 11.6 %copy-start.9 = (f32[256]{0:T(256)S(1)}, f32[256]{0:T(256)}, u32[]{:S(2)}) copy-start(f32[256]{0:T(256)} %param.29) | copy-start | bytes 3076
  134.9 11.6 %copy-start.10 = (f32[256]{0:T(256)S(1)}, f32[256]{0:T(256)}, u32[]{:S(2)}) copy-start(f32[256]{0:T(256)} %param.27) | copy-start | bytes 3076
  166.5 1.2 copy-start.3
  166.5 1.2 copy-start.6
  166.5 1.2 copy-start.11
where the time goes:
time: 172 us; the launch traced here: 171 us
  blocking collectives  83.4 us (48%)
  matrix products  26.2 us (15%)
  starting transfers between devices  19.9 us (12%)
  waiting for transfers between devices  18.1 us (11%)
  other arithmetic  17.2 us (10%)
  local copies, waits for them, and re-layouts  5.49 us (3%)
    all_to_all x1, blocking collectives, shards(): lax.all_to_all(row_remote, 'res', split_axis=2, concat_axis=0, tiled=True)  36.8 us
    all_to_all x1, blocking collectives, shards(): lax.all_to_all(col_split, 'seq', split_axis=1, concat_axis=0, tiled=True)  30.3 us
    all_to_all x1, starting transfers between devices, shards(): lax.all_to_all(row_split, 'res', split_axis=0, concat_axis=2, tiled=True)  19.9 us
    all_to_all x1, waiting for transfers between devices, shards(): lax.all_to_all(row_split, 'res', split_axis=0, concat_axis=2, tiled=True)  18.1 us
    all_to_all x1, blocking collectives, shards(): lax.all_to_all(col_remote.astype(jnp.bfloat16), 'seq', split_axis=0, conc...  16.3 us
    dot_general x16, matrix products, one_head(): jnp.einsum('nqd,nkd->nqk', query_head, key_head, preferred_element_type=j...  8.46 us
    dot_general x16, matrix products, one_head(): jnp.einsum('nqk,nkd->nqd', probabilities, value_head, preferred_element_t...  8.12 us
    reduce_sum x16, other arithmetic, one_head(): row_total = jnp.sum(weights, axis=-1, keepdims=True)  5.91 us
  transfers between devices with their start and end apart: 1, of which 1 were waited for; matrix products, arithmetic and copies ran while one was open for 0% of the time, Pallas kernels for 0%

commit v1 on v0

v1 whole, which is shorter than its diff:
```python
import functools

import jax
import jax.numpy as jnp
from jax import lax
from jax.experimental import pallas as pl
from jax.experimental.pallas import tpu as pltpu
from jax.sharding import PartitionSpec as P

HEADS = 8
LANES = 128
EPSILON = 1e-05
LOG2E = 1.4426950408889634
VMEM_LIMIT = 48 * 1024 * 1024


def normalize(values, gain, shift):
    row_mean = jnp.mean(values, axis=-1, keepdims=True)
    centred = values - row_mean
    variance = jnp.mean(centred * centred, axis=-1, keepdims=True)
    return (centred * lax.rsqrt(variance + EPSILON) * gain + shift).astype(jnp.bfloat16)


def matmul(left, right):
    return jnp.dot(left, right, preferred_element_type=jnp.float32)


def norm_kernel(values_ref, gain_ref, shift_ref, out_ref):
    out_ref[...] = normalize(values_ref[...], gain_ref[0:1], shift_ref[0:1])


def attention_kernel(normed_ref, entry_ref, gate_ref, out_ref, query_ref, key_ref, value_ref, gated_ref):
    rows, channels = normed_ref.shape
    head_size = channels // HEADS
    per_tile = LANES // head_size
    block = 256
    normed = normed_ref[...]
    query_ref[...] = (
        matmul(normed, entry_ref[:, :channels]) * (LOG2E * head_size**-0.5)
    ).astype(jnp.bfloat16)
    key_ref[...] = matmul(normed, entry_ref[:, channels : 2 * channels]).astype(jnp.bfloat16)
    value_ref[...] = matmul(normed, entry_ref[:, 2 * channels : 3 * channels]).astype(jnp.bfloat16)
    gated_ref[...] = jax.nn.sigmoid(matmul(normed, entry_ref[:, 3 * channels :]) + gate_ref[...])
    lane_head = lax.broadcasted_iota(jnp.int32, (1, LANES), 1) // head_size
    for tile in range(channels // LANES):
        lanes = slice(tile * LANES, (tile + 1) * LANES)
        keys = key_ref[:, lanes]
        values = jnp.concatenate(
            [value_ref[:, lanes], jnp.ones((rows, LANES), jnp.bfloat16)], axis=1
        )
        for start in range(0, rows, block):
            queries = query_ref[start : start + block, lanes]
            mixed = jnp.zeros((block, LANES), jnp.float32)
            for head in range(per_tile):
                mask = (lane_head == head).astype(jnp.float32)
                scores = lax.dot_general(
                    queries * mask.astype(jnp.bfloat16),
                    keys,
                    (((1,), (1,)), ((), ())),
                    preferred_element_type=jnp.float32,
                )
                peak = jnp.max(scores, axis=-1, keepdims=True)
                weights = jnp.exp2(scores - peak).astype(jnp.bfloat16)
                result = matmul(weights, values)
                mixed = jnp.where(lane_head == head, result[:, :LANES] / result[:, LANES:], mixed)
            out_ref[start : start + block, lanes] = (
                gated_ref[start : start + block, lanes] * mixed
            ).astype(jnp.bfloat16)


def turn_kernel(
    residues, base_ref, gated_ref, exit_ref, offset_ref, gain_ref, shift_ref, after_ref, out_ref, after_rows_ref
):
    rows = base_ref.shape[0]
    seqs = rows // residues
    after = base_ref[...] + (matmul(gated_ref[...], exit_ref[...]) + offset_ref[...])
    tiles = range(after_rows_ref.shape[0])
    for tile in tiles:
        after_rows_ref[tile] = after[:, tile * LANES : (tile + 1) * LANES]
    for item in range(residues):
        picked = jnp.concatenate(
            [after_rows_ref.at[tile][pl.ds(item, seqs, stride=residues), :] for tile in tiles], axis=1
        )
        after_ref[item * seqs : (item + 1) * seqs, :] = picked
        out_ref[item * seqs : (item + 1) * seqs, :] = normalize(picked, gain_ref[1:2], shift_ref[1:2])


def transition_kernel(
    residues,
    after_ref,
    gated_ref,
    exit_ref,
    offset_ref,
    gain_ref,
    shift_ref,
    first_ref,
    first_offset_ref,
    second_ref,
    second_offset_ref,
    out_ref,
    final_ref,
):
    rows = after_ref.shape[0]
    seqs = rows // residues
    group = 4
    block = group * seqs
    for start in range(0, rows, block):
        span = slice(start, start + block)
        after = after_ref[span, :] + (matmul(gated_ref[span, :], exit_ref[...]) + offset_ref[...])
        normed = normalize(after, gain_ref[2:3], shift_ref[2:3])
        inner = jnp.maximum(matmul(normed, first_ref[...]) + first_offset_ref[...], 0.0).astype(
            jnp.bfloat16
        )
        final = after + (matmul(inner, second_ref[...]) + second_offset_ref[...])
        for item in range(group):
            for tile in range(final_ref.shape[0]):
                final_ref.at[tile][pl.ds(start // seqs + item, seqs, stride=residues), :] = final[
                    item * seqs : (item + 1) * seqs, tile * LANES : (tile + 1) * LANES
                ]
    for tile in range(final_ref.shape[0]):
        out_ref[:, tile * LANES : (tile + 1) * LANES] = final_ref[tile]


def call(kernel, out_shape, scratch=(), flops=0, transcendentals=0, name=None):
    return pl.pallas_call(
        kernel,
        out_shape=out_shape,
        scratch_shapes=list(scratch),
        compiler_params=pltpu.CompilerParams(vmem_limit_bytes=VMEM_LIMIT),
        cost_estimate=pl.CostEstimate(
            flops=flops, bytes_accessed=2**21, transcendentals=transcendentals
        ),
        name=name,
    )


def attention(normed, entry, gate_offset):
    rows, channels = normed.shape
    return call(
        attention_kernel,
        jax.ShapeDtypeStruct((rows, channels), jnp.bfloat16),
        [pltpu.VMEM((rows, channels), jnp.bfloat16)] * 3 + [pltpu.VMEM((rows, channels), jnp.float32)],
        flops=8 * rows * channels * channels + 4 * rows * rows * channels,
        transcendentals=HEADS * rows * rows,
        name="attention",
    )(normed, entry, gate_offset.reshape(1, channels))


def exchange(values, axis):
    count = lax.axis_size(axis)
    rows, channels = values.shape
    return lax.all_to_all(
        values.reshape(count, rows // count, channels), axis, split_axis=0, concat_axis=0, tiled=True
    ).reshape(rows, channels)


def shards(
    alignment_tensor,
    standardizer_factors,
    standardizer_offsets,
    horizontal_entry_matrix,
    horizontal_sigmoid_offset,
    horizontal_exit_matrix,
    horizontal_exit_offset,
    vertical_entry_matrix,
    vertical_sigmoid_offset,
    vertical_exit_matrix,
    vertical_exit_offset,
    feedforward_first_matrix,
    feedforward_first_offset,
    feedforward_second_matrix,
    feedforward_second_offset,
):
    seq_local, res_local, channels = alignment_tensor.shape
    rows = seq_local * res_local
    base = alignment_tensor.reshape(rows, channels)
    narrow = jax.ShapeDtypeStruct((rows, channels), jnp.bfloat16)
    wide = jax.ShapeDtypeStruct((rows, channels), jnp.float32)
    row_normed = call(norm_kernel, narrow, name="row_norm")(
        base, standardizer_factors, standardizer_offsets
    )
    row_gated = attention(
        exchange(row_normed, "res"), horizontal_entry_matrix, horizontal_sigmoid_offset
    )
    after_row, col_normed = call(
        functools.partial(turn_kernel, res_local),
        (wide, narrow),
        [pltpu.VMEM((channels // LANES, rows, LANES), jnp.float32)],
        flops=2 * rows * channels * channels,
        name="after_row",
    )(
        base,
        exchange(row_gated, "res"),
        horizontal_exit_matrix,
        horizontal_exit_offset.reshape(1, channels),
        standardizer_factors,
        standardizer_offsets,
    )
    col_gated = attention(exchange(col_normed, "seq"), vertical_entry_matrix, vertical_sigmoid_offset)
    updated = call(
        functools.partial(transition_kernel, res_local),
        wide,
        [pltpu.VMEM((channels // LANES, rows, LANES), jnp.float32)],
        flops=18 * rows * channels * channels,
        name="transition",
    )(
        after_row,
        exchange(col_gated, "seq"),
        vertical_exit_matrix,
        vertical_exit_offset.reshape(1, channels),
        standardizer_factors,
        standardizer_offsets,
        feedforward_first_matrix,
        feedforward_first_offset.reshape(1, -1),
        feedforward_second_matrix,
        feedforward_second_offset.reshape(1, channels),
    )
    return updated.reshape(seq_local, res_local, channels)


def solution(mesh):
    return jax.shard_map(
        shards,
        mesh=mesh,
        in_specs=(P("seq", "res", None),) + (P(),) * 14,
        out_specs=P("seq", "res", None),
        check_vma=False,
    )
```

time: 172 us -> 127 us (0.74)
  the two profiles are of different devices: /device:TPU:16 before, /device:TPU:1 now
where the time goes in v1:
time: 127 us; the launch traced here: 124 us
  blocking collectives  103 us (81%)
  Pallas kernels  16.1 us (13%)
  local copies, waits for them, and re-layouts  5.24 us (4%)
    all_to_all x4, blocking collectives, exchange(): lax.all_to_all(values.reshape(count, rows // count, channels), axis, spli...  103 us
    pallas_call x2, Pallas kernels, attention(): call(attention_kernel, jax.ShapeDtypeStruct((rows, channels), jnp.bfloat1...  12.1 us
    unnamed x36, local copies, waits for them, and re-layouts  5.24 us
    pallas_call x1, Pallas kernels, shards(): call(functools.partial(transition_kernel, res_local), wide, [pltpu.VMEM((...  3.11 us

profile of v1, /device:TPU:1, one launch (start us, length us, event | category | flops | bytes accessed | tf_op | source)
XLA Modules:
  0.0 124.2 jit_solution(16694371538055850614)
XLA Ops:
  0.0 1.1 copy-done
  1.1 0.7 copy-done.3
  1.8 0.7 copy-done.5
  2.5 0.3 row_norm.1
  2.8 0.0 copy-start.8
  2.8 38.4 %all_to_all.20 = bf16[48,16,256]{2,1,0:T(8,128)(2,1)S(1)} all-to-all(bf16[48,16,256]{2,1,0:T(8,128)(2,1)S(1)} %bitcast.19), channel_id=1, replica_groups=mesh['seq'=16,'res'=48] {'res'}, dimensions={0} | all-to-all | bytes 786432 | tf_op jit(solution)/shard_map/all_to_all | solution.py:152
  41.3 0.7 copy-done.14
  41.9 6.0 %attention.2 = bf16[768,256]{1,0:T(8,128)(2,1)S(1)} custom-call(bf16[768,256]{1,0:T(8,128)(2,1)S(1)} %bitcast.22, bf16[256,1024]{1,0:T(8,128)(2,1)S(1)} %copy-done.8, f32[1,256]{1,0:T(1,128)S(1)} %bitcast.28), custom_call_target="tpu_custom_call" | custom-call | flops 1006632960 | bytes 2097152 | tf_op jit(solution)/shard_map/attention/pallas_call | solution.py:139
  48.0 0.0 copy-start.1
  48.0 0.0 copy-start.4
  48.0 28.1 %all_to_all.21 = bf16[48,16,256]{2,1,0:T(8,128)(2,1)S(1)} all-to-all(bf16[48,16,256]{2,1,0:T(8,128)(2,1)S(1)} %bitcast.23), channel_id=1, replica_groups=mesh['seq'=16,'res'=48] {'res'}, dimensions={0} | all-to-all | bytes 786432 | tf_op jit(solution)/shard_map/all_to_all | solution.py:152
  76.1 0.7 copy-done.7
  76.8 0.7 after_row.1
  77.5 0.0 copy-start.9
  77.5 20.5 %all_to_all.22 = bf16[16,48,256]{2,1,0:T(8,128)(2,1)S(1)} all-to-all(bf16[16,48,256]{2,1,0:T(8,128)(2,1)S(1)} %bitcast.20), channel_id=1, replica_groups=mesh['seq'=16,'res'=48] {'seq'}, dimensions={0} | all-to-all | bytes 786432 | tf_op jit(solution)/shard_map/all_to_all | solution.py:152
  98.0 0.7 copy-done.15
  98.6 6.0 %attention.3 = bf16[768,256]{1,0:T(8,128)(2,1)S(1)} custom-call(bf16[768,256]{1,0:T(8,128)(2,1)S(1)} %bitcast.24, bf16[256,1024]{1,0:T(8,128)(2,1)S(1)} %copy-done.9, f32[1,256]{1,0:T(1,128)S(1)} %bitcast.29), custom_call_target="tpu_custom_call" | custom-call | flops 1006632960 | bytes 2097152 | tf_op jit(solution)/shard_map/attention/pallas_call | solution.py:139
  104.7 0.0 copy-start.10
  104.7 0.0 copy-start.12
  104.7 0.0 copy-start.17
  104.7 15.6 %all_to_all.23 = bf16[16,48,256]{2,1,0:T(8,128)(2,1)S(1)} all-to-all(bf16[16,48,256]{2,1,0:T(8,128)(2,1)S(1)} %bitcast.25), channel_id=1, replica_groups=mesh['seq'=16,'res'=48] {'seq'}, dimensions={0} | all-to-all | bytes 786432 | tf_op jit(solution)/shard_map/all_to_all | solution.py:152
  120.4 0.7 copy-done.13
  121.0 0.0 copy-done.16
  121.0 3.1 %transition.1 = f32[768,256]{1,0:T(8,128)} custom-call(f32[768,256]{1,0:T(8,128)S(1)} %get-tuple-element.7.after_ref, bf16[768,256]{1,0:T(8,128)(2,1)S(1)} %bitcast.21, bf16[256,256]{1,0:T(8,128)(2,1)S(1)} %copy-done.12, f32[1,256]{1,0:T(1,128)S(1)} %bitcast.30, f32[3,256]{1,0:T(4,128)S(1)} %copy-done.4, f32[3,256]{1,0:T(4,128)S(1)} %copy-done.6, ...), custom_call_target="tpu_custom_call" | custom-call | flops 905969664 | bytes 2097152 | tf_op jit(solution)/shard_map/transition/pallas_call | solution.py:200
  (21 shorter events, 0.0 us)
Async XLA Ops:
  0.0 1.1 copy-start
  1.1 0.7 copy-start.3
  1.8 0.7 copy-start.5
  2.8 38.4 %copy-start.8 = (bf16[256,1024]{1,0:T(8,128)(2,1)S(1)}, bf16[256,1024]{1,0:T(8,128)(2,1)}, u32[]{:S(2)}) copy-start(bf16[256,1024]{1,0:T(8,128)(2,1)} %entry_ref.2) | copy-start | bytes 1572868
  41.2 0.7 copy-start.14
  41.9 34.2 %copy-start.2 = (bf16[256,256]{1,0:T(8,128)(2,1)S(1)}, bf16[256,256]{1,0:T(8,128)(2,1)}, u32[]{:S(2)}) copy-start(bf16[256,256]{1,0:T(8,128)(2,1)} %exit_ref.2) | copy-start | bytes 393220
  41.9 34.2 %copy-start.6 = (f32[3,256]{1,0:T(4,128)S(1)}, f32[3,256]{1,0:T(4,128)}, u32[]{:S(2)}) copy-start(f32[3,256]{1,0:T(4,128)} %shift_ref.5) | copy-start | bytes 9220
  48.0 28.2 %copy-start.1 = (f32[48,16,256]{2,1,0:T(8,128)S(1)}, f32[48,16,256]{2,1,0:T(8,128)}, u32[]{:S(2)}) copy-start(f32[48,16,256]{2,1,0:T(8,128)} %param.15) | copy-start | bytes 2359300
  48.0 28.2 %copy-start.4 = (f32[3,256]{1,0:T(4,128)S(1)}, f32[3,256]{1,0:T(4,128)}, u32[]{:S(2)}) copy-start(f32[3,256]{1,0:T(4,128)} %gain_ref.5) | copy-start | bytes 9220
  76.1 0.7 copy-start.7
  77.5 20.5 %copy-start.9 = (bf16[256,1024]{1,0:T(8,128)(2,1)S(1)}, bf16[256,1024]{1,0:T(8,128)(2,1)}, u32[]{:S(2)}) copy-start(bf16[256,1024]{1,0:T(8,128)(2,1)} %entry_ref.3) | copy-start | bytes 1572868
  98.0 0.7 copy-start.15
  98.6 21.7 %copy-start.11 = (bf16[1024,256]{1,0:T(8,128)(2,1)S(1)}, bf16[1024,256]{1,0:T(8,128)(2,1)}, u32[]{:S(2)}) copy-start(bf16[1024,256]{1,0:T(8,128)(2,1)} %second_ref.1) | copy-start | bytes 1572868
  104.7 15.7 %copy-start.10 = (bf16[256,1024]{1,0:T(8,128)(2,1)S(1)}, bf16[256,1024]{1,0:T(8,128)(2,1)}, u32[]{:S(2)}) copy-start(bf16[256,1024]{1,0:T(8,128)(2,1)} %first_ref.1) | copy-start | bytes 1572868
  104.7 15.7 %copy-start.12 = (bf16[256,256]{1,0:T(8,128)(2,1)S(1)}, bf16[256,256]{1,0:T(8,128)(2,1)}, u32[]{:S(2)}) copy-start(bf16[256,256]{1,0:T(8,128)(2,1)} %exit_ref.3) | copy-start | bytes 393220
  104.7 15.7 %copy-start.17 = (f32[256]{0:T(256)S(1)}, f32[256]{0:T(256)}, u32[]{:S(2)}) copy-start(f32[256]{0:T(256)} %param.29) | copy-start | bytes 3076
  120.4 0.7 copy-start.13
  120.4 0.7 copy-start.16

commit v2 on v1

v2 whole, which is shorter than its diff:
```python
import functools

import jax
import jax.numpy as jnp
from jax import lax
from jax.experimental import pallas as pl
from jax.experimental.pallas import tpu as pltpu
from jax.sharding import Mesh
from jax.sharding import PartitionSpec as P

HEADS = 8
CORES = 2
LANES = 128
BLOCK = 256
EPSILON = 1e-05
LOG2E = 1.4426950408889634
VMEM_LIMIT = 48 * 1024 * 1024
WHOLE_VMEM = 63 * 1024 * 1024

GAIN, SHIFT, ROW_GATE, ROW_EXIT, COL_GATE, COL_EXIT, SECOND, FIRST = 0, 3, 6, 7, 8, 9, 10, 12
PACKED = 16


def normalize(values, gain, shift):
    row_mean = jnp.mean(values, axis=-1, keepdims=True)
    centred = values - row_mean
    variance = jnp.mean(centred * centred, axis=-1, keepdims=True)
    return (centred * lax.rsqrt(variance + EPSILON) * gain + shift).astype(jnp.bfloat16)


def matmul(left, right):
    return jnp.dot(left, right, preferred_element_type=jnp.float32)


def centre_kernel(*refs):
    places = (GAIN, SHIFT, ROW_GATE, ROW_EXIT, COL_GATE, COL_EXIT, SECOND, FIRST)
    small = len(places)
    base_hbm, small_hbm = refs[0], refs[1 : 1 + small]
    out_ref, packed_ref, base_ref = refs[1 + small : 4 + small]
    small_refs, base_sem, small_sem = refs[4 + small : 4 + 2 * small], refs[-2], refs[-1]
    rows, channels = base_ref.shape
    parts = base_sem.shape[0]
    part = rows // parts
    copies = [
        pltpu.make_async_copy(
            base_hbm.at[pl.ds(i * part, part)], base_ref.at[pl.ds(i * part, part)], base_sem.at[i]
        )
        for i in range(parts)
    ]
    for copy in copies:
        copy.start()
    small_copies = [
        pltpu.make_async_copy(small_hbm[i], small_refs[i], small_sem.at[i]) for i in range(small)
    ]
    for copy in small_copies:
        copy.start()
    for i in range(parts):
        copies[i].wait()
        values = base_ref[i * part : (i + 1) * part]
        out_ref[i * part : (i + 1) * part] = (
            values - jnp.mean(values, axis=-1, keepdims=True)
        ).astype(jnp.bfloat16)
    packed_ref[...] = jnp.zeros_like(packed_ref)
    for i, place in enumerate(places):
        small_copies[i].wait()
        count, width = small_refs[i].shape
        for j in range(count):
            for k in range(width // channels):
                row = place + j + k
                packed_ref[row : row + 1] = small_refs[i][j : j + 1, k * channels : (k + 1) * channels]


def project(normed, entry_ref, gate, query_ref, key_ref, value_ref, gate_ref):
    channels = normed.shape[1]
    scale = LOG2E * (channels // HEADS) ** -0.5
    query_ref[...] = (matmul(normed, entry_ref[:, :channels]) * scale).astype(jnp.bfloat16)
    key_ref[...] = matmul(normed, entry_ref[:, channels : 2 * channels]).astype(jnp.bfloat16)
    value = matmul(normed, entry_ref[:, 2 * channels : 3 * channels]).astype(jnp.bfloat16)
    for tile in range(channels // LANES):
        value_ref[tile, :, :LANES] = value[:, tile * LANES : (tile + 1) * LANES]
        value_ref[tile, :, LANES:] = jnp.ones((normed.shape[0], LANES), jnp.bfloat16)
    gate_ref[...] = jax.nn.sigmoid(matmul(normed, entry_ref[:, 3 * channels :]) + gate)


def attend(span, query_ref, key_ref, value_ref, gate_ref):
    channels = query_ref.shape[1]
    head_size = channels // HEADS
    lane_head = lax.broadcasted_iota(jnp.int32, (1, LANES), 1) // head_size
    gated = []
    for tile in range(channels // LANES):
        lanes = slice(tile * LANES, (tile + 1) * LANES)
        queries = query_ref[span, lanes]
        keys = key_ref[:, lanes]
        mixed = jnp.zeros(queries.shape, jnp.float32)
        for head in range(LANES // head_size):
            mask = (lane_head == head).astype(jnp.float32)
            scores = lax.dot_general(
                queries * mask.astype(jnp.bfloat16),
                keys,
                (((1,), (1,)), ((), ())),
                preferred_element_type=jnp.float32,
            )
            peak = jnp.max(scores, axis=-1, keepdims=True)
            weights = jnp.exp2(scores - peak).astype(jnp.bfloat16)
            result = matmul(weights, value_ref[tile])
            mixed = jnp.where(lane_head == head, result[:, :LANES] / result[:, LANES:], mixed)
        gated.append((gate_ref[span, lanes] * mixed).astype(jnp.bfloat16))
    return jnp.concatenate(gated, axis=1)


def row_kernel(
    columns, residual_ref, entry_ref, exit_ref, packed_ref, out_ref, query_ref, key_ref, value_ref, gate_ref, after_ref
):
    rows = residual_ref.shape[0]
    normed = normalize(
        residual_ref[...].astype(jnp.float32), packed_ref[GAIN : GAIN + 1], packed_ref[SHIFT : SHIFT + 1]
    )
    work = (query_ref, key_ref, value_ref, gate_ref)
    project(normed, entry_ref, packed_ref[ROW_GATE : ROW_GATE + 1], *work)
    tiles = range(after_ref.shape[0])
    for start in range(0, rows, BLOCK):
        span = slice(start, min(start + BLOCK, rows))
        after = residual_ref[span, :].astype(jnp.float32) + (
            matmul(attend(span, *work), exit_ref[...]) + packed_ref[ROW_EXIT : ROW_EXIT + 1]
        )
        for tile in tiles:
            after_ref[tile, span, :] = after[:, tile * LANES : (tile + 1) * LANES]
    stride = CORES * columns
    chips = rows // stride
    pair = 2
    for first in range(0, stride, pair):
        for tile in tiles:
            picked = [
                after_ref.at[tile][pl.ds(first + i, chips, stride=stride), :] for i in range(pair)
            ]
            out_ref[first * chips : (first + pair) * chips, tile * LANES : (tile + 1) * LANES] = (
                jnp.concatenate(picked, axis=0).astype(jnp.bfloat16)
            )


def interleave_kernel(values_ref, out_ref, mixed_ref):
    rows = values_ref.shape[0]
    half = rows // CORES
    for tile in range(mixed_ref.shape[0]):
        lanes = slice(tile * LANES, (tile + 1) * LANES)
        for core in range(CORES):
            mixed_ref.at[tile][pl.ds(core, half, stride=CORES), :] = values_ref[
                core * half : (core + 1) * half, lanes
            ].astype(jnp.float32)
        out_ref[:, lanes] = mixed_ref[tile].astype(jnp.bfloat16)


def col_kernel(
    residual_ref,
    entry_ref,
    exit_ref,
    first_ref,
    second_ref,
    packed_ref,
    out_ref,
    query_ref,
    key_ref,
    value_ref,
    gate_ref,
):
    rows, channels = residual_ref.shape
    normed = normalize(
        residual_ref[...].astype(jnp.float32),
        packed_ref[GAIN + 1 : GAIN + 2],
        packed_ref[SHIFT + 1 : SHIFT + 2],
    )
    work = (query_ref, key_ref, value_ref, gate_ref)
    project(normed, entry_ref, packed_ref[COL_GATE : COL_GATE + 1], *work)
    for start in range(0, rows, BLOCK):
        span = slice(start, min(start + BLOCK, rows))
        after = residual_ref[span, :].astype(jnp.float32) + (
            matmul(attend(span, *work), exit_ref[...]) + packed_ref[COL_EXIT : COL_EXIT + 1]
        )
        normed = normalize(after, packed_ref[GAIN + 2 : GAIN + 3], packed_ref[SHIFT + 2 : SHIFT + 3])
        update = packed_ref[SECOND : SECOND + 1]
        for part in range(first_ref.shape[1] // channels):
            hidden = slice(part * channels, (part + 1) * channels)
            inner = jnp.maximum(
                matmul(normed, first_ref[:, hidden]) + packed_ref[FIRST + part : FIRST + part + 1], 0.0
            )
            update = update + matmul(inner.astype(jnp.bfloat16), second_ref[hidden, :])
        out_ref[span, :] = (after + update).astype(jnp.bfloat16)


def home_kernel(residues, base_ref, values_ref, out_ref, turned_ref):
    rows = base_ref.shape[0]
    seqs = rows // residues
    for tile in range(turned_ref.shape[0]):
        lanes = slice(tile * LANES, (tile + 1) * LANES)
        for item in range(residues):
            turned_ref.at[tile][pl.ds(item, seqs, stride=residues), :] = values_ref[
                item * seqs : (item + 1) * seqs, lanes
            ].astype(jnp.float32)
    mean = jnp.mean(base_ref[...], axis=-1, keepdims=True)
    for tile in range(turned_ref.shape[0]):
        out_ref[:, tile * LANES : (tile + 1) * LANES] = turned_ref[tile] + mean


def call(
    kernel, out_shape, scratch=(), flops=0, transcendentals=0, name=None, vmem=VMEM_LIMIT, **specs
):
    return pl.pallas_call(
        kernel,
        out_shape=out_shape,
        scratch_shapes=list(scratch),
        compiler_params=pltpu.CompilerParams(vmem_limit_bytes=vmem),
        cost_estimate=pl.CostEstimate(
            flops=flops, bytes_accessed=2**21, transcendentals=transcendentals
        ),
        name=name,
        **specs,
    )


def exchange(values, axes):
    count = lax.axis_size(axes)
    rows, channels = values.shape
    return lax.all_to_all(
        values.reshape(count, rows // count, channels), axes, split_axis=0, concat_axis=0, tiled=True
    ).reshape(rows, channels)


def shards(
    alignment_tensor,
    standardizer_factors,
    standardizer_offsets,
    horizontal_entry_matrix,
    horizontal_sigmoid_offset,
    horizontal_exit_matrix,
    horizontal_exit_offset,
    vertical_entry_matrix,
    vertical_sigmoid_offset,
    vertical_exit_matrix,
    vertical_exit_offset,
    feedforward_first_matrix,
    feedforward_first_offset,
    feedforward_second_matrix,
    feedforward_second_offset,
):
    seq_local, res_local, channels = alignment_tensor.shape
    rows = seq_local * res_local
    base = alignment_tensor.reshape(rows, channels)
    narrow = jax.ShapeDtypeStruct((rows, channels), jnp.bfloat16)
    wide = jax.ShapeDtypeStruct((rows, channels), jnp.float32)
    split = pltpu.VMEM((channels // LANES, rows, LANES), jnp.float32)
    work = [
        pltpu.VMEM((rows, channels), jnp.bfloat16),
        pltpu.VMEM((rows, channels), jnp.bfloat16),
        pltpu.VMEM((channels // LANES, rows, 2 * LANES), jnp.bfloat16),
        pltpu.VMEM((rows, channels), jnp.float32),
    ]
    exps = HEADS * rows * rows
    attention_flops = 10 * rows * channels * channels + 4 * rows * rows * channels
    small = [
        standardizer_factors,
        standardizer_offsets,
        horizontal_sigmoid_offset.reshape(1, -1),
        horizontal_exit_offset.reshape(1, -1),
        vertical_sigmoid_offset.reshape(1, -1),
        vertical_exit_offset.reshape(1, -1),
        feedforward_second_offset.reshape(1, -1),
        feedforward_first_offset.reshape(1, -1),
    ]
    vmem = pl.BlockSpec(memory_space=pltpu.VMEM)
    centred, packed = call(
        centre_kernel,
        (narrow, jax.ShapeDtypeStruct((PACKED, channels), jnp.float32)),
        [pltpu.VMEM((rows, channels), jnp.float32)]
        + [pltpu.VMEM(array.shape, jnp.float32) for array in small]
        + [pltpu.SemaphoreType.DMA((4,)), pltpu.SemaphoreType.DMA((len(small),))],
        name="centre",
        vmem=WHOLE_VMEM,
        in_specs=[pl.BlockSpec(memory_space=pltpu.HBM)] * (1 + len(small)),
        out_specs=(vmem, vmem),
    )(base, *small)
    after_row = call(
        functools.partial(row_kernel, res_local),
        narrow,
        work + [split],
        flops=attention_flops,
        transcendentals=exps,
        name="row_attention",
    )(
        exchange(centred, ("chip", "core")),
        horizontal_entry_matrix,
        horizontal_exit_matrix,
        packed,
    )
    by_chip = call(interleave_kernel, narrow, [split], name="interleave")(exchange(after_row, "core"))
    updated = call(
        col_kernel,
        narrow,
        work,
        flops=attention_flops + 16 * rows * channels * channels,
        transcendentals=exps,
        name="col_attention_transition",
    )(
        exchange(by_chip, ("seq", "chip")),
        vertical_entry_matrix,
        vertical_exit_matrix,
        feedforward_first_matrix,
        feedforward_second_matrix,
        packed,
    )
    home = call(functools.partial(home_kernel, res_local), wide, [split], name="home")(
        base, exchange(updated, "seq")
    )
    return home.reshape(seq_local, res_local, channels)


def solution(mesh):
    seq_count, res_count = mesh.devices.shape
    cut = Mesh(mesh.devices.reshape(seq_count, res_count // CORES, CORES), ("seq", "chip", "core"))
    placed = P("seq", ("chip", "core"), None)
    return jax.shard_map(
        shards, mesh=cut, in_specs=(placed,) + (P(),) * 14, out_specs=placed, check_vma=False
    )
```

time: 127 us -> 122 us (0.961); the launches traced: 124 us -> 121 us
  Pallas kernels: 16.1 us -> 20.6 us
  blocking collectives: 103 us -> 98.9 us
  local copies, waits for them, and re-layouts: 5.24 us -> 1.2 us
    pallas_call x5, Pallas kernels: 16.1 us -> 20.6 us  [the longest x1 9.02 us: shards(): call(col_kernel, narrow, work, flops=attention_flops + 16 * rows * channe...]
    unnamed x36 -> x16, local copies, waits for them, and re-layouts: 5.24 us -> 0.9 us
    all_to_all x4, blocking collectives: 103 us -> 98.9 us  [exchange(): lax.all_to_all(values.reshape(count, rows // count, channels), axes, spli...]
where the time goes in v2:
time: 122 us; the launch traced here: 121 us
  blocking collectives  98.9 us (81%)
  Pallas kernels  20.6 us (17%)
    all_to_all x4, blocking collectives, exchange(): lax.all_to_all(values.reshape(count, rows // count, channels), axes, spli...  98.9 us
    pallas_call x1, Pallas kernels, shards(): call(col_kernel, narrow, work, flops=attention_flops + 16 * rows * channe...  9.02 us
    pallas_call x1, Pallas kernels, shards(): call(functools.partial(row_kernel, res_local), narrow, work + [split], fl...  8 us

profile of v2, /device:TPU:1, one launch (start us, length us, event | category | flops | bytes accessed | tf_op | source)
XLA Modules:
  0.0 120.9 jit_solution(1695791610817632143)
XLA Ops:
  0.0 2.3 %centre.1 = (bf16[768,256]{1,0:T(8,128)(2,1)}, f32[16,256]{1,0:T(8,128)}) custom-call(f32[768,256]{1,0:T(8,128)} %bitcast.14, f32[3,256]{1,0:T(4,128)} %refs_1_.1, f32[3,256]{1,0:T(4,128)} %refs_2_.1, f32[1,256]{1,0:T(1,128)} %bitcast.23, f32[1,256]{1,0:T(1,128)} %bitcast.24, f32[1,256]{1,0:T(1,128)} %bitcast.25, f32[1,256]{1,0:T(1,128)} %bitcast.26, ...), custom_call_target="tpu_custom_call" | custom-call | bytes 2097152 | tf_op jit(solution)/shard_map/centre/pallas_call | solution.py:270
  2.3 0.0 copy-start.1
  2.3 0.0 copy-start.5
  2.3 0.0 copy-start.7
  2.3 38.6 %all_to_all.20 = bf16[48,16,256]{2,1,0:T(8,128)(2,1)S(1)} all-to-all(bf16[48,16,256]{2,1,0:T(8,128)(2,1)} %bitcast.21), channel_id=1, replica_groups=mesh['seq'=16,'chip'=24,'core'=2] {'chip','core'}, dimensions={0} | all-to-all | bytes 786432 | tf_op jit(solution)/shard_map/all_to_all | solution.py:223
  40.9 0.0 copy-done.1
  41.0 0.0 copy-done.5
  41.0 8.0 %row_attention.1 = bf16[768,256]{1,0:T(8,128)(2,1)S(1)} custom-call(bf16[768,256]{1,0:T(8,128)(2,1)S(1)} %bitcast.18, bf16[256,1024]{1,0:T(8,128)(2,1)S(1)} %copy-done.1, bf16[256,256]{1,0:T(8,128)(2,1)S(1)} %copy-done.5, f32[16,256]{1,0:T(8,128)S(1)} %copy-done.7), custom_call_target="tpu_custom_call" | custom-call | flops 1107296256 | bytes 2097152 | tf_op jit(solution)/shard_map/row_attention/pallas_call | solution.py:281
  49.0 4.4 %all_to_all.21 = bf16[2,384,256]{2,1,0:T(8,128)(2,1)S(1)} all-to-all(bf16[2,384,256]{2,1,0:T(8,128)(2,1)S(1)} %bitcast.20), channel_id=1, replica_groups=mesh['seq'=16,'chip'=24,'core'=2] {'core'}, dimensions={0} | all-to-all | bytes 786432 | tf_op jit(solution)/shard_map/all_to_all | solution.py:223
  53.4 0.1 interleave.1
  53.5 0.0 copy-start.6
  53.5 0.2 reshape.59
  53.6 0.0 copy-start.3
  53.7 0.0 copy-start.4
  53.7 42.3 %all_to_all.22 = bf16[384,2,256]{2,1,0:T(2,128)(2,1)S(1)} all-to-all(bf16[384,2,256]{2,1,0:T(2,128)(2,1)S(1)} %reshape.59), channel_id=1, replica_groups=mesh['seq'=16,'chip'=24,'core'=2] {'seq','chip'}, dimensions={0} | all-to-all | bytes 786432 | tf_op jit(solution)/shard_map/all_to_all | solution.py:223
  95.9 0.2 reshape.60.residual_ref
  96.1 0.0 copy-done.6
  96.1 0.0 copy-done.3
  96.1 0.0 copy-done.4
  96.1 0.9 copy-done.2
  97.0 9.0 %col_attention_transition.1 = bf16[768,256]{1,0:T(8,128)(2,1)S(1)} custom-call(bf16[768,256]{1,0:T(8,128)(2,1)S(1)} %reshape.60.residual_ref, bf16[256,1024]{1,0:T(8,128)(2,1)S(1)} %copy-done.2, bf16[256,256]{1,0:T(8,128)(2,1)S(1)} %copy-done.6, bf16[256,1024]{1,0:T(8,128)(2,1)S(1)} %copy-done.3, bf16[1024,256]{1,0:T(8,128)(2,1)S(1)} %copy-done.4, ...), custom_call_target="tpu_custom_call" | custom-call | flops 1912602624 | bytes 2097152 | tf_op jit(solution)/shard_map/col_attention_transition/pallas_call | solution.py:295
  106.0 0.0 copy-start
  106.0 13.6 %all_to_all.23 = bf16[16,48,256]{2,1,0:T(8,128)(2,1)S(1)} all-to-all(bf16[16,48,256]{2,1,0:T(8,128)(2,1)S(1)} %bitcast.19), channel_id=1, replica_groups=mesh['seq'=16,'chip'=24,'core'=2] {'seq'}, dimensions={0} | all-to-all | bytes 786432 | tf_op jit(solution)/shard_map/all_to_all | solution.py:223
  119.7 1.2 %home.1 = f32[768,256]{1,0:T(8,128)} custom-call(f32[768,256]{1,0:T(8,128)S(1)} %bitcast.15, bf16[768,256]{1,0:T(8,128)(2,1)S(1)} %bitcast.17), custom_call_target="tpu_custom_call" | custom-call | bytes 2097152 | tf_op jit(solution)/shard_map/home/pallas_call | solution.py:310
  (3 shorter events, 0.0 us)
Async XLA Ops:
  2.3 38.7 %copy-start.1 = (bf16[256,1024]{1,0:T(8,128)(2,1)S(1)}, bf16[256,1024]{1,0:T(8,128)(2,1)}, u32[]{:S(2)}) copy-start(bf16[256,1024]{1,0:T(8,128)(2,1)} %entry_ref.2) | copy-start | bytes 1572868
  2.3 38.6 %copy-start.5 = (bf16[256,256]{1,0:T(8,128)(2,1)S(1)}, bf16[256,256]{1,0:T(8,128)(2,1)}, u32[]{:S(2)}) copy-start(bf16[256,256]{1,0:T(8,128)(2,1)} %exit_ref.2) | copy-start | bytes 393220
  2.3 38.6 %copy-start.7 = (f32[16,256]{1,0:T(8,128)S(1)}, f32[16,256]{1,0:T(8,128)}, u32[]{:S(2)}) copy-start(f32[16,256]{1,0:T(8,128)} %get-tuple-element.8.packed_ref) | copy-start | bytes 49156
  53.5 42.6 %copy-start.6 = (bf16[256,256]{1,0:T(8,128)(2,1)S(1)}, bf16[256,256]{1,0:T(8,128)(2,1)}, u32[]{:S(2)}) copy-start(bf16[256,256]{1,0:T(8,128)(2,1)} %exit_ref.3) | copy-start | bytes 393220
  53.6 42.5 %copy-start.3 = (bf16[256,1024]{1,0:T(8,128)(2,1)S(1)}, bf16[256,1024]{1,0:T(8,128)(2,1)}, u32[]{:S(2)}) copy-start(bf16[256,1024]{1,0:T(8,128)(2,1)} %first_ref.1) | copy-start | bytes 1572868
  53.7 42.5 %copy-start.4 = (bf16[1024,256]{1,0:T(8,128)(2,1)S(1)}, bf16[1024,256]{1,0:T(8,128)(2,1)}, u32[]{:S(2)}) copy-start(bf16[1024,256]{1,0:T(8,128)(2,1)} %second_ref.1) | copy-start | bytes 1572868
  95.9 1.0 copy-start.2
  106.0 13.7 %copy-start = (f32[48,16,256]{2,1,0:T(8,128)S(1)}, f32[48,16,256]{2,1,0:T(8,128)}, u32[]{:S(2)}) copy-start(f32[48,16,256]{2,1,0:T(8,128)} %param.15) | copy-start | bytes 2359300

commit v3 on v2

--- a/solution.py
+++ b/solution.py
@@ -9,13 +9,15 @@
 from jax.sharding import PartitionSpec as P
 
 HEADS = 8
-CORES = 2
+X, Z_LOW, Z_HIGH, CORES = 4, 4, 3, 2
 LANES = 128
-BLOCK = 256
+PROJECT_ROWS, QUERY_ROWS = 256, 768
 EPSILON = 1e-05
 LOG2E = 1.4426950408889634
 VMEM_LIMIT = 48 * 1024 * 1024
 WHOLE_VMEM = 63 * 1024 * 1024
+
+SEQ = ("x", "z_low")
 
 GAIN, SHIFT, ROW_GATE, ROW_EXIT, COL_GATE, COL_EXIT, SECOND, FIRST = 0, 3, 6, 7, 8, 9, 10, 12
 PACKED = 16
@@ -32,15 +34,22 @@
     return jnp.dot(left, right, preferred_element_type=jnp.float32)
 
 
-def centre_kernel(*refs):
+def by_device(block):
+    y, rest = divmod(block, Z_HIGH * CORES)
+    z_high, core = divmod(rest, CORES)
+    return (y * CORES + core) * Z_HIGH + z_high
+
+
+def centre_kernel(columns, *refs):
     places = (GAIN, SHIFT, ROW_GATE, ROW_EXIT, COL_GATE, COL_EXIT, SECOND, FIRST)
     small = len(places)
     base_hbm, small_hbm = refs[0], refs[1 : 1 + small]
-    out_ref, packed_ref, base_ref = refs[1 + small : 4 + small]
-    small_refs, base_sem, small_sem = refs[4 + small : 4 + 2 * small], refs[-2], refs[-1]
+    out_hbm, packed_ref, base_ref, out_ref = refs[1 + small : 5 + small]
+    small_refs, (base_sem, out_sem, small_sem) = refs[5 + small : 5 + 2 * small], refs[-3:]
     rows, channels = base_ref.shape
     parts = base_sem.shape[0]
     part = rows // parts
+    assert part % (columns * Z_HIGH * CORES) == 0
     copies = [
         pltpu.make_async_copy(
             base_hbm.at[pl.ds(i * part, part)], base_ref.at[pl.ds(i * part, part)], base_sem.at[i]
@@ -54,12 +63,20 @@
     ]
     for copy in small_copies:
         copy.start()
+    out_copies = [
+        pltpu.make_async_copy(
+            out_ref.at[pl.ds(i * part, part)], out_hbm.at[pl.ds(i * part, part)], out_sem.at[i]
+        )
+        for i in range(parts)
+    ]
     for i in range(parts):
         copies[i].wait()
         values = base_ref[i * part : (i + 1) * part]
-        out_ref[i * part : (i + 1) * part] = (
-            values - jnp.mean(values, axis=-1, keepdims=True)
-        ).astype(jnp.bfloat16)
+        centred = (values - jnp.mean(values, axis=-1, keepdims=True)).astype(jnp.bfloat16)
+        for first in range(0, part, columns):
+            place = by_device((i * part + first) // columns) * columns
+            out_ref[place : place + columns] = centred[first : first + columns]
+        out_copies[i].start()
     packed_ref[...] = jnp.zeros_like(packed_ref)
     for i, place in enumerate(places):
         small_copies[i].wait()
@@ -68,18 +85,26 @@
             for k in range(width // channels):
                 row = place + j + k
                 packed_ref[row : row + 1] = small_refs[i][j : j + 1, k * channels : (k + 1) * channels]
-
-
-def project(normed, entry_ref, gate, query_ref, key_ref, value_ref, gate_ref):
-    channels = normed.shape[1]
+    for copy in out_copies:
+        copy.wait()
+
+
+def spans(rows, block):
+    return [slice(start, min(start + block, rows)) for start in range(0, rows, block)]
+
+
+def project(residual_ref, entry_ref, gain, shift, gate, query_ref, key_ref, value_ref, gate_ref):
+    rows, channels = residual_ref.shape
     scale = LOG2E * (channels // HEADS) ** -0.5
-    query_ref[...] = (matmul(normed, entry_ref[:, :channels]) * scale).astype(jnp.bfloat16)
-    key_ref[...] = matmul(normed, entry_ref[:, channels : 2 * channels]).astype(jnp.bfloat16)
-    value = matmul(normed, entry_ref[:, 2 * channels : 3 * channels]).astype(jnp.bfloat16)
-    for tile in range(channels // LANES):
-        value_ref[tile, :, :LANES] = value[:, tile * LANES : (tile + 1) * LANES]
-        value_ref[tile, :, LANES:] = jnp.ones((normed.shape[0], LANES), jnp.bfloat16)
-    gate_ref[...] = jax.nn.sigmoid(matmul(normed, entry_ref[:, 3 * channels :]) + gate)
+    for span in spans(rows, PROJECT_ROWS):
+        normed = normalize(residual_ref[span, :].astype(jnp.float32), gain, shift)
+        query_ref[span, :] = (matmul(normed, entry_ref[:, :channels]) * scale).astype(jnp.bfloat16)
+        key_ref[span, :] = matmul(normed, entry_ref[:, channels : 2 * channels]).astype(jnp.bfloat16)
+        value = matmul(normed, entry_ref[:, 2 * channels : 3 * channels]).astype(jnp.bfloat16)
+        for tile in range(channels // LANES):
+            value_ref[tile, span, :LANES] = value[:, tile * LANES : (tile + 1) * LANES]
+            value_ref[tile, span, LANES:] = jnp.ones((normed.shape[0], LANES), jnp.bfloat16)
+        gate_ref[span, :] = jax.nn.sigmoid(matmul(normed, entry_ref[:, 3 * channels :]) + gate)
 
 
 def attend(span, query_ref, key_ref, value_ref, gate_ref):
@@ -108,71 +133,55 @@
     return jnp.concatenate(gated, axis=1)
 
 
-def row_kernel(
-    columns, residual_ref, entry_ref, exit_ref, packed_ref, out_ref, query_ref, key_ref, value_ref, gate_ref, after_ref
-):
+def row_kernel(columns, residual_ref, entry_ref, exit_ref, packed_ref, out_ref, *work):
     rows = residual_ref.shape[0]
-    normed = normalize(
-        residual_ref[...].astype(jnp.float32), packed_ref[GAIN : GAIN + 1], packed_ref[SHIFT : SHIFT + 1]
-    )
-    work = (query_ref, key_ref, value_ref, gate_ref)
-    project(normed, entry_ref, packed_ref[ROW_GATE : ROW_GATE + 1], *work)
-    tiles = range(after_ref.shape[0])
-    for start in range(0, rows, BLOCK):
-        span = slice(start, min(start + BLOCK, rows))
+    project(
+        residual_ref,
+        entry_ref,
+        packed_ref[GAIN : GAIN + 1],
+        packed_ref[SHIFT : SHIFT + 1],
+        packed_ref[ROW_GATE : ROW_GATE + 1],
+        *work,
+    )
+    for span in spans(rows, QUERY_ROWS):
         after = residual_ref[span, :].astype(jnp.float32) + (
             matmul(attend(span, *work), exit_ref[...]) + packed_ref[ROW_EXIT : ROW_EXIT + 1]
         )
-        for tile in tiles:
-            after_ref[tile, span, :] = after[:, tile * LANES : (tile + 1) * LANES]
-    stride = CORES * columns
-    chips = rows // stride
-    pair = 2
-    for first in range(0, stride, pair):
-        for tile in tiles:
-            picked = [
-                after_ref.at[tile][pl.ds(first + i, chips, stride=stride), :] for i in range(pair)
-            ]
-            out_ref[first * chips : (first + pair) * chips, tile * LANES : (tile + 1) * LANES] = (
-                jnp.concatenate(picked, axis=0).astype(jnp.bfloat16)
-            )
-
-
-def interleave_kernel(values_ref, out_ref, mixed_ref):
+        after = after.astype(jnp.bfloat16)
+        for first in range(span.start, span.stop, columns):
+            y, rest = divmod(first // columns, CORES * Z_HIGH)
+            core, z_high = divmod(rest, Z_HIGH)
+            place = core * (rows // CORES) + (y * Z_HIGH + z_high) * columns
+            out_ref[place : place + columns, :] = after[first - span.start : first - span.start + columns]
+
+
+def turn_kernel(columns, values_ref, *refs):
+    out_ref, turned_ref = refs[-2:]
     rows = values_ref.shape[0]
     half = rows // CORES
-    for tile in range(mixed_ref.shape[0]):
+    chips = half // columns
+    for tile in range(turned_ref.shape[0]):
         lanes = slice(tile * LANES, (tile + 1) * LANES)
         for core in range(CORES):
-            mixed_ref.at[tile][pl.ds(core, half, stride=CORES), :] = values_ref[
-                core * half : (core + 1) * half, lanes
-            ].astype(jnp.float32)
-        out_ref[:, lanes] = mixed_ref[tile].astype(jnp.bfloat16)
-
-
-def col_kernel(
-    residual_ref,
-    entry_ref,
-    exit_ref,
-    first_ref,
-    second_ref,
-    packed_ref,
-    out_ref,
-    query_ref,
-    key_ref,
-    value_ref,
-    gate_ref,
-):
+            values = values_ref[core * half : (core + 1) * half, lanes].astype(jnp.float32)
+            for chip in range(chips):
+                turned_ref.at[tile][pl.ds(chip * CORES + core, columns, stride=CORES * chips), :] = (
+                    values[chip * columns : (chip + 1) * columns]
+                )
+        out_ref[:, lanes] = turned_ref[tile].astype(jnp.bfloat16)
+
+
+def col_kernel(residual_ref, entry_ref, exit_ref, first_ref, second_ref, packed_ref, out_ref, *work):
     rows, channels = residual_ref.shape
-    normed = normalize(
-        residual_ref[...].astype(jnp.float32),
+    project(
+        residual_ref,
+        entry_ref,
         packed_ref[GAIN + 1 : GAIN + 2],
         packed_ref[SHIFT + 1 : SHIFT + 2],
-    )
-    work = (query_ref, key_ref, value_ref, gate_ref)
-    project(normed, entry_ref, packed_ref[COL_GATE : COL_GATE + 1], *work)
-    for start in range(0, rows, BLOCK):
-        span = slice(start, min(start + BLOCK, rows))
+        packed_ref[COL_GATE : COL_GATE + 1],
+        *work,
+    )
+    for span in spans(rows, QUERY_ROWS):
         after = residual_ref[span, :].astype(jnp.float32) + (
             matmul(attend(span, *work), exit_ref[...]) + packed_ref[COL_EXIT : COL_EXIT + 1]
         )
@@ -244,6 +253,7 @@
 ):
     seq_local, res_local, channels = alignment_tensor.shape
     rows = seq_local * res_local
+    seq_count = lax.axis_size(SEQ)
     base = alignment_tensor.reshape(rows, channels)
     narrow = jax.ShapeDtypeStruct((rows, channels), jnp.bfloat16)
     wide = jax.ShapeDtypeStruct((rows, channels), jnp.float32)
@@ -266,32 +276,42 @@
         feedforward_second_offset.reshape(1, -1),
         feedforward_first_offset.reshape(1, -1),
     ]
+    parts = max(rows // (2 * seq_count * Z_HIGH * CORES), 1)
     vmem = pl.BlockSpec(memory_space=pltpu.VMEM)
+    hbm = pl.BlockSpec(memory_space=pltpu.HBM)
     centred, packed = call(
-        centre_kernel,
+        functools.partial(centre_kernel, seq_count),
         (narrow, jax.ShapeDtypeStruct((PACKED, channels), jnp.float32)),
-        [pltpu.VMEM((rows, channels), jnp.float32)]
+        [pltpu.VMEM((rows, channels), jnp.float32), pltpu.VMEM((rows, channels), jnp.bfloat16)]
         + [pltpu.VMEM(array.shape, jnp.float32) for array in small]
-        + [pltpu.SemaphoreType.DMA((4,)), pltpu.SemaphoreType.DMA((len(small),))],
+        + [pltpu.SemaphoreType.DMA((count,)) for count in (parts, parts, len(small))],
         name="centre",
         vmem=WHOLE_VMEM,
-        in_specs=[pl.BlockSpec(memory_space=pltpu.HBM)] * (1 + len(small)),
-        out_specs=(vmem, vmem),
+        in_specs=[hbm] * (1 + len(small)),
+        out_specs=(hbm, vmem),
     )(base, *small)
     after_row = call(
-        functools.partial(row_kernel, res_local),
+        functools.partial(row_kernel, seq_count),
         narrow,
-        work + [split],
+        work,
         flops=attention_flops,
         transcendentals=exps,
         name="row_attention",
     )(
-        exchange(centred, ("chip", "core")),
+        exchange(centred, ("y", "core", "z_high")),
         horizontal_entry_matrix,
         horizontal_exit_matrix,
         packed,
     )
-    by_chip = call(interleave_kernel, narrow, [split], name="interleave")(exchange(after_row, "core"))
+    col_weights = (
+        vertical_entry_matrix,
+        vertical_exit_matrix,
+        feedforward_first_matrix,
+        feedforward_second_matrix,
+    )
+    by_chip = call(functools.partial(turn_kernel, seq_count), narrow, [split], name="turn")(
+        exchange(after_row, "core"), *col_weights
+    )
     updated = call(
         col_kernel,
         narrow,
@@ -300,23 +320,20 @@
         transcendentals=exps,
         name="col_attention_transition",
     )(
-        exchange(by_chip, ("seq", "chip")),
-        vertical_entry_matrix,
-        vertical_exit_matrix,
-        feedforward_first_matrix,
-        feedforward_second_matrix,
+        exchange(by_chip, SEQ + ("y", "z_high")),
+        *col_weights,
         packed,
     )
     home = call(functools.partial(home_kernel, res_local), wide, [split], name="home")(
-        base, exchange(updated, "seq")
+        base, exchange(updated, SEQ)
     )
     return home.reshape(seq_local, res_local, channels)
 
 
 def solution(mesh):
-    seq_count, res_count = mesh.devices.shape
-    cut = Mesh(mesh.devices.reshape(seq_count, res_count // CORES, CORES), ("seq", "chip", "core"))
-    placed = P("seq", ("chip", "core"), None)
+    axes = ("z_low", "x", "z_high", "y", "core")
+    cut = Mesh(mesh.devices.reshape(Z_LOW, X, Z_HIGH, -1, CORES), axes)
+    placed = P(axes[:2], axes[2:], None)
     return jax.shard_map(
         shards, mesh=cut, in_specs=(placed,) + (P(),) * 14, out_specs=placed, check_vma=False
     )

time: 122 us -> 122 us (level)
  blocking collectives: 98.9 us -> 102 us
  Pallas kernels: 20.6 us -> 19.1 us
    all_to_all x4, blocking collectives: 98.9 us -> 102 us  [exchange(): lax.all_to_all(values.reshape(count, rows // count, channels), axes, spli...]
where the time goes in v3:
time: 122 us
  blocking collectives  102 us (84%)
  Pallas kernels  19.1 us (16%)
    all_to_all x4, blocking collectives, exchange(): lax.all_to_all(values.reshape(count, rows // count, channels), axes, spli...  102 us
    pallas_call x1, Pallas kernels, shards(): call(col_kernel, narrow, work, flops=attention_flops + 16 * rows * channe...  7.89 us
    pallas_call x1, Pallas kernels, shards(): call(functools.partial(row_kernel, seq_count), narrow, work, flops=attent...  6.87 us
    pallas_call x1, Pallas kernels, shards(): call(functools.partial(centre_kernel, seq_count), (narrow, jax.ShapeDtype...  2.79 us

profile of v3, /device:TPU:1, one launch (start us, length us, event | category | flops | bytes accessed | tf_op | source)
XLA Modules:
  0.0 121.8 jit_solution(6635384168961802760)
XLA Ops:
  0.0 2.8 %centre.1 = (bf16[768,256]{1,0:T(8,128)(2,1)}, f32[16,256]{1,0:T(8,128)}) custom-call(f32[768,256]{1,0:T(8,128)} %bitcast.14, f32[3,256]{1,0:T(4,128)} %refs_1_.2, f32[3,256]{1,0:T(4,128)} %refs_2_.2, f32[1,256]{1,0:T(1,128)} %bitcast.23, f32[1,256]{1,0:T(1,128)} %bitcast.24, f32[1,256]{1,0:T(1,128)} %bitcast.25, f32[1,256]{1,0:T(1,128)} %bitcast.26, ...), custom_call_target="tpu_custom_call" | custom-call | bytes 2097152 | tf_op jit(solution)/shard_map/centre/pallas_call | solution.py:282
  2.8 0.0 copy-start.5
  2.8 0.0 copy-start.6
  2.8 0.0 copy-start.7
  2.8 40.7 %all_to_all.20 = bf16[48,16,256]{2,1,0:T(8,128)(2,1)S(1)} all-to-all(bf16[48,16,256]{2,1,0:T(8,128)(2,1)} %bitcast.21), channel_id=1, replica_groups=mesh['z_low'=4,'x'=4,'z_high'=3,'y'=8,'core'=2] {'y','core','z_high'}, dimensions={0} | all-to-all | bytes 786432 | tf_op jit(solution)/shard_map/all_to_all | solution.py:232
  43.6 0.0 copy-done.5
  43.6 0.0 copy-done.6
  43.6 0.0 copy-done.7
  43.6 0.0 copy-start.2
  43.6 0.0 copy-start.3
  43.6 6.9 %row_attention.1 = bf16[768,256]{1,0:T(8,128)(2,1)S(1)} custom-call(bf16[768,256]{1,0:T(8,128)(2,1)S(1)} %bitcast.18, bf16[256,1024]{1,0:T(8,128)(2,1)S(1)} %copy-done.5, bf16[256,256]{1,0:T(8,128)(2,1)S(1)} %copy-done.6, f32[16,256]{1,0:T(8,128)S(1)} %copy-done.7), custom_call_target="tpu_custom_call" | custom-call | flops 1107296256 | bytes 2097152 | tf_op jit(solution)/shard_map/row_attention/pallas_call | solution.py:293
  50.5 0.0 copy-start.1
  50.5 0.0 copy-start.4
  50.5 3.9 %all_to_all.21 = bf16[2,384,256]{2,1,0:T(8,128)(2,1)S(1)} all-to-all(bf16[2,384,256]{2,1,0:T(8,128)(2,1)S(1)} %bitcast.20), channel_id=1, replica_groups=mesh['z_low'=4,'x'=4,'z_high'=3,'y'=8,'core'=2] {'core'}, dimensions={0} | all-to-all | bytes 786432 | tf_op jit(solution)/shard_map/all_to_all | solution.py:232
  54.4 0.0 copy-done.2
  54.4 0.0 copy-done.3
  54.4 0.3 turn.1
  54.7 0.2 reshape.59
  54.9 42.0 %all_to_all.22 = bf16[384,2,256]{2,1,0:T(2,128)(2,1)S(1)} all-to-all(bf16[384,2,256]{2,1,0:T(2,128)(2,1)S(1)} %reshape.59), channel_id=1, replica_groups=mesh['z_low'=4,'x'=4,'z_high'=3,'y'=8,'core'=2] {'x','z_low','y','z_high'}, dimensions={0} | all-to-all | bytes 786432 | tf_op jit(solution)/shard_map/all_to_all | solution.py:232
  96.9 0.2 reshape.60.residual_ref
  97.0 7.9 %col_attention_transition.1 = bf16[768,256]{1,0:T(8,128)(2,1)S(1)} custom-call(bf16[768,256]{1,0:T(8,128)(2,1)S(1)} %reshape.60.residual_ref, bf16[256,1024]{1,0:T(8,128)(2,1)S(1)} %copy-done.1, bf16[256,256]{1,0:T(8,128)(2,1)S(1)} %copy-done.4, bf16[256,1024]{1,0:T(8,128)(2,1)S(1)} %copy-done.2, bf16[1024,256]{1,0:T(8,128)(2,1)S(1)} %copy-done.3, ...), custom_call_target="tpu_custom_call" | custom-call | flops 1912602624 | bytes 2097152 | tf_op jit(solution)/shard_map/col_attention_transition/pallas_call | solution.py:315
  104.9 0.0 copy-start
  104.9 15.6 %all_to_all.23 = bf16[16,48,256]{2,1,0:T(8,128)(2,1)S(1)} all-to-all(bf16[16,48,256]{2,1,0:T(8,128)(2,1)S(1)} %bitcast.19), channel_id=1, replica_groups=mesh['z_low'=4,'x'=4,'z_high'=3,'y'=8,'core'=2] {'x','z_low'}, dimensions={0} | all-to-all | bytes 786432 | tf_op jit(solution)/shard_map/all_to_all | solution.py:232
  120.5 1.2 home.1
  (3 shorter events, 0.0 us)
Async XLA Ops:
  2.8 40.8 %copy-start.5 = (bf16[256,1024]{1,0:T(8,128)(2,1)S(1)}, bf16[256,1024]{1,0:T(8,128)(2,1)}, u32[]{:S(2)}) copy-start(bf16[256,1024]{1,0:T(8,128)(2,1)} %entry_ref.2) | copy-start | bytes 1572868
  2.8 40.8 %copy-start.6 = (bf16[256,256]{1,0:T(8,128)(2,1)S(1)}, bf16[256,256]{1,0:T(8,128)(2,1)}, u32[]{:S(2)}) copy-start(bf16[256,256]{1,0:T(8,128)(2,1)} %exit_ref.2) | copy-start | bytes 393220
  2.8 40.8 %copy-start.7 = (f32[16,256]{1,0:T(8,128)S(1)}, f32[16,256]{1,0:T(8,128)}, u32[]{:S(2)}) copy-start(f32[16,256]{1,0:T(8,128)} %get-tuple-element.8.packed_ref) | copy-start | bytes 49156
  43.6 10.8 %copy-start.2 = (bf16[256,1024]{1,0:T(8,128)(2,1)S(1)}, bf16[256,1024]{1,0:T(8,128)(2,1)}, u32[]{:S(2)}) copy-start(bf16[256,1024]{1,0:T(8,128)(2,1)} %first_ref.1) | copy-start | bytes 1572868
  43.6 10.8 %copy-start.3 = (bf16[1024,256]{1,0:T(8,128)(2,1)S(1)}, bf16[1024,256]{1,0:T(8,128)(2,1)}, u32[]{:S(2)}) copy-start(bf16[1024,256]{1,0:T(8,128)(2,1)} %second_ref.1) | copy-start | bytes 1572868
  50.5 3.9 %copy-start.1 = (bf16[256,1024]{1,0:T(8,128)(2,1)S(1)}, bf16[256,1024]{1,0:T(8,128)(2,1)}, u32[]{:S(2)}) copy-start(bf16[256,1024]{1,0:T(8,128)(2,1)} %entry_ref.3) | copy-start | bytes 1572868
  50.5 3.9 %copy-start.4 = (bf16[256,256]{1,0:T(8,128)(2,1)S(1)}, bf16[256,256]{1,0:T(8,128)(2,1)}, u32[]{:S(2)}) copy-start(bf16[256,256]{1,0:T(8,128)(2,1)} %exit_ref.3) | copy-start | bytes 393220
  104.9 15.6 %copy-start = (f32[48,16,256]{2,1,0:T(8,128)S(1)}, f32[48,16,256]{2,1,0:T(8,128)}, u32[]{:S(2)}) copy-start(f32[48,16,256]{2,1,0:T(8,128)} %param.15) | copy-start | bytes 2359300

commit v4 on v3

--- a/solution.py
+++ b/solution.py
@@ -17,7 +17,7 @@
 VMEM_LIMIT = 48 * 1024 * 1024
 WHOLE_VMEM = 63 * 1024 * 1024
 
-SEQ = ("x", "z_low")
+SEQ = ("z_low", "x")
 
 GAIN, SHIFT, ROW_GATE, ROW_EXIT, COL_GATE, COL_EXIT, SECOND, FIRST = 0, 3, 6, 7, 8, 9, 10, 12
 PACKED = 16
@@ -44,8 +44,8 @@
     places = (GAIN, SHIFT, ROW_GATE, ROW_EXIT, COL_GATE, COL_EXIT, SECOND, FIRST)
     small = len(places)
     base_hbm, small_hbm = refs[0], refs[1 : 1 + small]
-    out_hbm, packed_ref, base_ref, out_ref = refs[1 + small : 5 + small]
-    small_refs, (base_sem, out_sem, small_sem) = refs[5 + small : 5 + 2 * small], refs[-3:]
+    out_ref, packed_ref, base_ref = refs[1 + small : 4 + small]
+    small_refs, (base_sem, small_sem) = refs[4 + small : 4 + 2 * small], refs[-2:]
     rows, channels = base_ref.shape
     parts = base_sem.shape[0]
     part = rows // parts
@@ -63,12 +63,6 @@
     ]
     for copy in small_copies:
         copy.start()
-    out_copies = [
-        pltpu.make_async_copy(
-            out_ref.at[pl.ds(i * part, part)], out_hbm.at[pl.ds(i * part, part)], out_sem.at[i]
-        )
-        for i in range(parts)
-    ]
     for i in range(parts):
         copies[i].wait()
         values = base_ref[i * part : (i + 1) * part]
@@ -76,7 +70,6 @@
         for first in range(0, part, columns):
             place = by_device((i * part + first) // columns) * columns
             out_ref[place : place + columns] = centred[first : first + columns]
-        out_copies[i].start()
     packed_ref[...] = jnp.zeros_like(packed_ref)
     for i, place in enumerate(places):
         small_copies[i].wait()
@@ -85,8 +78,6 @@
             for k in range(width // channels):
                 row = place + j + k
                 packed_ref[row : row + 1] = small_refs[i][j : j + 1, k * channels : (k + 1) * channels]
-    for copy in out_copies:
-        copy.wait()
 
 
 def spans(rows, block):
@@ -107,20 +98,19 @@
         gate_ref[span, :] = jax.nn.sigmoid(matmul(normed, entry_ref[:, 3 * channels :]) + gate)
 
 
-def attend(span, query_ref, key_ref, value_ref, gate_ref):
-    channels = query_ref.shape[1]
+def attend(queries, gates, key_ref, value_ref):
+    channels = queries.shape[1]
     head_size = channels // HEADS
     lane_head = lax.broadcasted_iota(jnp.int32, (1, LANES), 1) // head_size
     gated = []
     for tile in range(channels // LANES):
         lanes = slice(tile * LANES, (tile + 1) * LANES)
-        queries = query_ref[span, lanes]
         keys = key_ref[:, lanes]
-        mixed = jnp.zeros(queries.shape, jnp.float32)
+        mixed = jnp.zeros((queries.shape[0], LANES), jnp.float32)
         for head in range(LANES // head_size):
             mask = (lane_head == head).astype(jnp.float32)
             scores = lax.dot_general(
-                queries * mask.astype(jnp.bfloat16),
+                queries[:, lanes] * mask.astype(jnp.bfloat16),
                 keys,
                 (((1,), (1,)), ((), ())),
                 preferred_element_type=jnp.float32,
@@ -129,12 +119,30 @@
             weights = jnp.exp2(scores - peak).astype(jnp.bfloat16)
             result = matmul(weights, value_ref[tile])
             mixed = jnp.where(lane_head == head, result[:, :LANES] / result[:, LANES:], mixed)
-        gated.append((gate_ref[span, lanes] * mixed).astype(jnp.bfloat16))
+        gated.append((gates[:, lanes] * mixed).astype(jnp.bfloat16))
     return jnp.concatenate(gated, axis=1)
 
 
-def row_kernel(columns, residual_ref, entry_ref, exit_ref, packed_ref, out_ref, *work):
-    rows = residual_ref.shape[0]
+def for_core(ref, columns, core):
+    size = Z_HIGH * columns
+    return jnp.concatenate(
+        [
+            ref[pl.ds(pl.multiple_of(first + core * size, columns), size), :]
+            for first in range(0, ref.shape[0], CORES * size)
+        ],
+        axis=0,
+    )
+
+
+def after_row(columns, core, residual_ref, exit_ref, packed_ref, query_ref, key_ref, value_ref, gate_ref):
+    gated = attend(
+        for_core(query_ref, columns, core), for_core(gate_ref, columns, core), key_ref, value_ref
+    )
+    update = matmul(gated, exit_ref[...]) + packed_ref[ROW_EXIT : ROW_EXIT + 1]
+    return (for_core(residual_ref, columns, core).astype(jnp.float32) + update).astype(jnp.bfloat16)
+
+
+def row_send_kernel(columns, core_ref, residual_ref, entry_ref, exit_ref, packed_ref, out_ref, *work):
     project(
         residual_ref,
         entry_ref,
@@ -143,27 +151,26 @@
         packed_ref[ROW_GATE : ROW_GATE + 1],
         *work,
     )
-    for span in spans(rows, QUERY_ROWS):
-        after = residual_ref[span, :].astype(jnp.float32) + (
-            matmul(attend(span, *work), exit_ref[...]) + packed_ref[ROW_EXIT : ROW_EXIT + 1]
-        )
-        after = after.astype(jnp.bfloat16)
-        for first in range(span.start, span.stop, columns):
-            y, rest = divmod(first // columns, CORES * Z_HIGH)
-            core, z_high = divmod(rest, Z_HIGH)
-            place = core * (rows // CORES) + (y * Z_HIGH + z_high) * columns
-            out_ref[place : place + columns, :] = after[first - span.start : first - span.start + columns]
-
-
-def turn_kernel(columns, values_ref, *refs):
+    out_ref[...] = after_row(columns, 1 - core_ref[0], residual_ref, exit_ref, packed_ref, *work)
+
+
+def row_keep_kernel(columns, core_ref, residual_ref, exit_ref, packed_ref, *refs):
+    *work, out_ref = refs
+    out_ref[...] = after_row(columns, core_ref[0], residual_ref, exit_ref, packed_ref, *work)
+
+
+def turn_kernel(columns, core_ref, kept_ref, received_ref, *refs):
     out_ref, turned_ref = refs[-2:]
-    rows = values_ref.shape[0]
-    half = rows // CORES
+    half = kept_ref.shape[0]
     chips = half // columns
+    own = jnp.full((1, LANES), core_ref[0], jnp.int32) == 0
     for tile in range(turned_ref.shape[0]):
         lanes = slice(tile * LANES, (tile + 1) * LANES)
-        for core in range(CORES):
-            values = values_ref[core * half : (core + 1) * half, lanes].astype(jnp.float32)
+        kept = kept_ref[:, lanes].astype(jnp.float32)
+        received = received_ref[:, lanes].astype(jnp.float32)
+        for core, values in enumerate(
+            (jnp.where(own, kept, received), jnp.where(own, received, kept))
+        ):
             for chip in range(chips):
                 turned_ref.at[tile][pl.ds(chip * CORES + core, columns, stride=CORES * chips), :] = (
                     values[chip * columns : (chip + 1) * columns]
@@ -181,9 +188,12 @@
         packed_ref[COL_GATE : COL_GATE + 1],
         *work,
     )
+    query_ref, key_ref, value_ref, gate_ref = work
     for span in spans(rows, QUERY_ROWS):
         after = residual_ref[span, :].astype(jnp.float32) + (
-            matmul(attend(span, *work), exit_ref[...]) + packed_ref[COL_EXIT : COL_EXIT + 1]
+            matmul(
+                attend(query_ref[span, :], gate_ref[span, :], key_ref, value_ref), exit_ref[...]
+            ) + packed_ref[COL_EXIT : COL_EXIT + 1]
         )
         normed = normalize(after, packed_ref[GAIN + 2 : GAIN + 3], packed_ref[SHIFT + 2 : SHIFT + 3])
         update = packed_ref[SECOND : SECOND + 1]
@@ -282,36 +292,51 @@
     centred, packed = call(
         functools.partial(centre_kernel, seq_count),
         (narrow, jax.ShapeDtypeStruct((PACKED, channels), jnp.float32)),
-        [pltpu.VMEM((rows, channels), jnp.float32), pltpu.VMEM((rows, channels), jnp.bfloat16)]
+        [pltpu.VMEM((rows, channels), jnp.float32)]
         + [pltpu.VMEM(array.shape, jnp.float32) for array in small]
-        + [pltpu.SemaphoreType.DMA((count,)) for count in (parts, parts, len(small))],
+        + [pltpu.SemaphoreType.DMA((count,)) for count in (parts, len(small))],
         name="centre",
         vmem=WHOLE_VMEM,
         in_specs=[hbm] * (1 + len(small)),
-        out_specs=(hbm, vmem),
+        out_specs=(vmem, vmem),
     )(base, *small)
-    after_row = call(
-        functools.partial(row_kernel, seq_count),
-        narrow,
-        work,
-        flops=attention_flops,
-        transcendentals=exps,
-        name="row_attention",
-    )(
-        exchange(centred, ("y", "core", "z_high")),
-        horizontal_entry_matrix,
-        horizontal_exit_matrix,
-        packed,
-    )
+    core = lax.axis_index("core").astype(jnp.int32).reshape(1)
+    smem = pl.BlockSpec(memory_space=pltpu.SMEM)
+    half = jax.ShapeDtypeStruct((rows // CORES, channels), jnp.bfloat16)
+    residual = exchange(centred, ("y", "core", "z_high"))
+    sent, *projected = call(
+        functools.partial(row_send_kernel, seq_count),
+        (half, *(jax.ShapeDtypeStruct(array.shape, array.dtype) for array in work)),
+        flops=attention_flops // 2,
+        transcendentals=exps // 2,
+        name="row_attention_send",
+        in_specs=[smem] + [vmem] * 4,
+        out_specs=(vmem,) * 5,
+    )(core, residual, horizontal_entry_matrix, horizontal_exit_matrix, packed)
+    received = lax.ppermute(sent, "core", [(i, CORES - 1 - i) for i in range(CORES)])
+    kept = call(
+        functools.partial(row_keep_kernel, seq_count),
+        half,
+        flops=attention_flops // 2,
+        transcendentals=exps // 2,
+        name="row_attention_keep",
+        in_specs=[smem] + [vmem] * 7,
+        out_specs=vmem,
+    )(core, residual, horizontal_exit_matrix, packed, *projected)
     col_weights = (
         vertical_entry_matrix,
         vertical_exit_matrix,
         feedforward_first_matrix,
         feedforward_second_matrix,
     )
-    by_chip = call(functools.partial(turn_kernel, seq_count), narrow, [split], name="turn")(
-        exchange(after_row, "core"), *col_weights
-    )
+    by_chip = call(
+        functools.partial(turn_kernel, seq_count),
+        narrow,
+        [split],
+        name="turn",
+        in_specs=[smem] + [vmem] * 6,
+        out_specs=vmem,
+    )(core, kept, received, *col_weights)
     updated = call(
         col_kernel,
         narrow,

time: 122 us -> 119 us (0.975)
  blocking collectives: 102 us -> 56.6 us
  starting transfers between devices: 0 us -> 23.2 us
  waiting for transfers between devices: 0 us -> 19.5 us
    all_to_all x4 -> x2, blocking collectives: 102 us -> 56.6 us  [exchange(): lax.all_to_all(values.reshape(count, rows // count, channels), axes, spli...]
    all_to_all x0 -> x1, starting transfers between devices: none -> 21.2 us  [exchange(): lax.all_to_all(values.reshape(count, rows // count, channels), axes, spli...]
    all_to_all x0 -> x1, waiting for transfers between devices: none -> 19.5 us  [exchange(): lax.all_to_all(values.reshape(count, rows // count, channels), axes, spli...]
    ppermute x0 -> x1, starting transfers between devices: none -> 2.02 us  [shards(): lax.ppermute(sent, 'core', [(i, CORES - 1 - i) for i in range(CORES)])]
    pallas_call x1 -> x2, Pallas kernels: 6.87 us -> 7.51 us  [the longest x1 4.2 us: shards(): call(functools.partial(row_send_kernel, seq_count), (half, *(jax.ShapeDty...]
  transfers between devices with their start and end apart: 0 -> 2, of which waited for: 0 -> 1; matrix products, arithmetic and copies ran while one was open for 0% -> 0% of each run, Pallas kernels for 0% -> 3%
where the time goes in v4:
time: 119 us
  blocking collectives  56.6 us (48%)
  starting transfers between devices  23.2 us (19%)
  waiting for transfers between devices  19.5 us (16%)
  Pallas kernels  19.2 us (16%)
    all_to_all x2, blocking collectives, exchange(): lax.all_to_all(values.reshape(count, rows // count, channels), axes, spli...  56.6 us
    all_to_all x1, starting transfers between devices, exchange(): lax.all_to_all(values.reshape(count, rows // count, channels), axes, spli...  21.2 us
    all_to_all x1, waiting for transfers between devices, exchange(): lax.all_to_all(values.reshape(count, rows // count, channels), axes, spli...  19.5 us
    pallas_call x1, Pallas kernels, shards(): call(col_kernel, narrow, work, flops=attention_flops + 16 * rows * channe...  7.9 us
    pallas_call x1, Pallas kernels, shards(): call(functools.partial(row_send_kernel, seq_count), (half, *(jax.ShapeDty...  4.2 us
    pallas_call x1, Pallas kernels, shards(): call(functools.partial(row_keep_kernel, seq_count), half, flops=attention...  3.31 us
  transfers between devices with their start and end apart: 2, of which 1 were waited for; matrix products, arithmetic and copies ran while one was open for 0% of the time, Pallas kernels for 3%

profile of v4, /device:TPU:1, one launch (start us, length us, event | category | flops | bytes accessed | tf_op | source)
XLA Modules:
  0.0 119.1 jit_solution(5000102105451229638)
XLA Ops:
  0.0 2.3 %centre.1 = (bf16[768,256]{1,0:T(8,128)(2,1)}, f32[16,256]{1,0:T(8,128)}) custom-call(f32[768,256]{1,0:T(8,128)} %bitcast.13, f32[3,256]{1,0:T(4,128)} %refs_1_.2, f32[3,256]{1,0:T(4,128)} %refs_2_.2, f32[1,256]{1,0:T(1,128)} %bitcast.21, f32[1,256]{1,0:T(1,128)} %bitcast.22, f32[1,256]{1,0:T(1,128)} %bitcast.23, f32[1,256]{1,0:T(1,128)} %bitcast.24, ...), custom_call_target="tpu_custom_call" | custom-call | bytes 2097152 | tf_op jit(solution)/shard_map/centre/pallas_call | solution.py:292
  2.3 0.0 copy-start.5
  2.3 0.0 copy-start.6
  2.3 21.2 %all-to-all-start = ((bf16[48,16,256]{2,1,0:T(8,128)(2,1)}), bf16[48,16,256]{2,1,0:T(8,128)(2,1)S(1)}, u32[]{:S(2)}, u32[]{:S(2)}) async-start(bf16[48,16,256]{2,1,0:T(8,128)(2,1)} %bitcast.19), calls=%async_computation | async-start | bytes 786432 | tf_op jit(solution)/shard_map/all_to_all | solution.py:242
  23.5 19.5 %all-to-all-done = bf16[48,16,256]{2,1,0:T(8,128)(2,1)S(1)} async-done(((bf16[48,16,256]{2,1,0:T(8,128)(2,1)}), bf16[48,16,256]{2,1,0:T(8,128)(2,1)S(1)}, u32[]{:S(2)}, u32[]{:S(2)}) %all-to-all-start) | async-done | bytes 393248 | tf_op jit(solution)/shard_map/all_to_all | solution.py:242
  43.1 0.0 copy-done.7
  43.1 4.2 %row_attention_send.1 = (bf16[384,256]{1,0:T(8,128)(2,1)S(1)}, bf16[768,256]{1,0:T(8,128)(2,1)S(1)}, bf16[768,256]{1,0:T(8,128)(2,1)S(1)}, bf16[2,768,256]{2,1,0:T(8,128)(2,1)S(1)}, f32[768,256]{1,0:T(8,128)S(1)}) custom-call(s32[1]{0:T(128)} %bitcast.1.core_ref, bf16[768,256]{1,0:T(8,128)(2,1)S(1)} %bitcast.16, bf16[256,1024]{1,0:T(8,128)(2,1)S(1)} %copy-done.5, ...), custom_call_target="tpu_custom_call" | custom-call | flops 553648128 | bytes 2097152 | tf_op jit(solution)/shard_map/row_attention_send/pallas_call | solution.py:307
  47.3 2.0 %collective-permute-start = (bf16[384,256]{1,0:T(8,128)(2,1)S(1)}, bf16[384,256]{1,0:T(8,128)(2,1)S(1)}, u32[]{:S(2)}, u32[]{:S(2)}) collective-permute-start(bf16[384,256]{1,0:T(8,128)(2,1)S(1)} %get-tuple-element.18), channel_id=1, source_target_pairs={{0,1},{1,0},{2,3},{3,2},{4,5},{5,4},{6,7},{7,6},{8,9},{9,8},{10,11... | collective-permute-start | bytes 589832 | tf_op jit(solution)/shard_map/ppermute | solution.py:316
  49.3 0.0 copy-start.1
  49.3 0.0 copy-start.2
  49.3 0.0 copy-start.3
  49.4 0.0 copy-start.4
  49.4 3.3 %row_attention_keep.1.kept_ref = bf16[384,256]{1,0:T(8,128)(2,1)S(1)} custom-call(s32[1]{0:T(128)} %bitcast.1.core_ref, bf16[768,256]{1,0:T(8,128)(2,1)S(1)} %bitcast.17, bf16[256,256]{1,0:T(8,128)(2,1)S(1)} %copy-done.6, f32[16,256]{1,0:T(8,128)S(1)} %copy-done.7, bf16[768,256]{1,0:T(8,128)(2,1)S(1)} %get-tuple-element.14.refs_0_, ...), custom_call_target="tpu_custom_call" | custom-call | flops 553648128 | bytes 2097152 | tf_op jit(solution)/shard_map/row_attention_keep/pallas_call | solution.py:317
  52.7 0.0 collective-permute-done.received_ref
  52.7 0.0 copy-done.1
  52.7 0.0 copy-done.2
  52.7 0.3 turn.1
  53.0 0.2 reshape.55
  53.2 42.1 %all_to_all.15 = bf16[384,2,256]{2,1,0:T(2,128)(2,1)S(1)} all-to-all(bf16[384,2,256]{2,1,0:T(2,128)(2,1)S(1)} %reshape.55), channel_id=1, replica_groups=mesh['z_low'=4,'x'=4,'z_high'=3,'y'=8,'core'=2] {'z_low','x','y','z_high'}, dimensions={0} | all-to-all | bytes 786432 | tf_op jit(solution)/shard_map/all_to_all | solution.py:242
  95.3 0.2 reshape.56.residual_ref
  95.4 7.9 %col_attention_transition.1 = bf16[768,256]{1,0:T(8,128)(2,1)S(1)} custom-call(bf16[768,256]{1,0:T(8,128)(2,1)S(1)} %reshape.56.residual_ref, bf16[256,1024]{1,0:T(8,128)(2,1)S(1)} %copy-done.1, bf16[256,256]{1,0:T(8,128)(2,1)S(1)} %copy-done.4, bf16[256,1024]{1,0:T(8,128)(2,1)S(1)} %copy-done.2, bf16[1024,256]{1,0:T(8,128)(2,1)S(1)} %copy-done.3, ...), custom_call_target="tpu_custom_call" | custom-call | flops 1912602624 | bytes 2097152 | tf_op jit(solution)/shard_map/col_attention_transition/pallas_call | solution.py:340
  103.3 0.0 copy-start
  103.3 14.6 %all_to_all.16 = bf16[16,48,256]{2,1,0:T(8,128)(2,1)S(1)} all-to-all(bf16[16,48,256]{2,1,0:T(8,128)(2,1)S(1)} %bitcast.18), channel_id=1, replica_groups=mesh['z_low'=4,'x'=4,'z_high'=3,'y'=8,'core'=2] {'z_low','x'}, dimensions={0} | all-to-all | bytes 786432 | tf_op jit(solution)/shard_map/all_to_all | solution.py:242
  117.9 1.2 %home.1 = f32[768,256]{1,0:T(8,128)} custom-call(f32[768,256]{1,0:T(8,128)S(1)} %bitcast.14, bf16[768,256]{1,0:T(8,128)(2,1)S(1)} %bitcast.15), custom_call_target="tpu_custom_call" | custom-call | bytes 2097152 | tf_op jit(solution)/shard_map/home/pallas_call | solution.py:352
  (6 shorter events, 0.0 us)
Async XLA Ops:
  2.3 40.8 %copy-start.5 = (bf16[256,1024]{1,0:T(8,128)(2,1)S(1)}, bf16[256,1024]{1,0:T(8,128)(2,1)}, u32[]{:S(2)}) copy-start(bf16[256,1024]{1,0:T(8,128)(2,1)} %entry_ref.2) | copy-start | bytes 1572868
  2.3 40.8 %copy-start.6 = (bf16[256,256]{1,0:T(8,128)(2,1)S(1)}, bf16[256,256]{1,0:T(8,128)(2,1)}, u32[]{:S(2)}) copy-start(bf16[256,256]{1,0:T(8,128)(2,1)} %exit_ref.4) | copy-start | bytes 393220
  2.3 40.8 %copy-start.7 = (f32[16,256]{1,0:T(8,128)S(1)}, f32[16,256]{1,0:T(8,128)}, u32[]{:S(2)}) copy-start(f32[16,256]{1,0:T(8,128)} %get-tuple-element.13.packed_ref) | copy-start | bytes 49156
  2.3 40.7 %all-to-all-start = ((bf16[48,16,256]{2,1,0:T(8,128)(2,1)}), bf16[48,16,256]{2,1,0:T(8,128)(2,1)S(1)}, u32[]{:S(2)}, u32[]{:S(2)}) async-start(bf16[48,16,256]{2,1,0:T(8,128)(2,1)} %bitcast.19), calls=%async_computation | async-start | bytes 786432 | tf_op jit(solution)/shard_map/all_to_all | solution.py:242
  47.3 5.4 %collective-permute-start = (bf16[384,256]{1,0:T(8,128)(2,1)S(1)}, bf16[384,256]{1,0:T(8,128)(2,1)S(1)}, u32[]{:S(2)}, u32[]{:S(2)}) collective-permute-start(bf16[384,256]{1,0:T(8,128)(2,1)S(1)} %get-tuple-element.18), channel_id=1, source_target_pairs={{0,1},{1,0},{2,3},{3,2},{4,5},{5,4},{6,7},{7,6},{8,9},{9,8},{10,11... | collective-permute-start | bytes 589832 | tf_op jit(solution)/shard_map/ppermute | solution.py:316
  49.3 3.4 %copy-start.1 = (bf16[256,1024]{1,0:T(8,128)(2,1)S(1)}, bf16[256,1024]{1,0:T(8,128)(2,1)}, u32[]{:S(2)}) copy-start(bf16[256,1024]{1,0:T(8,128)(2,1)} %entry_ref.3) | copy-start | bytes 1572868
  49.3 3.4 %copy-start.2 = (bf16[256,1024]{1,0:T(8,128)(2,1)S(1)}, bf16[256,1024]{1,0:T(8,128)(2,1)}, u32[]{:S(2)}) copy-start(bf16[256,1024]{1,0:T(8,128)(2,1)} %first_ref.1) | copy-start | bytes 1572868
  49.3 3.4 %copy-start.3 = (bf16[1024,256]{1,0:T(8,128)(2,1)S(1)}, bf16[1024,256]{1,0:T(8,128)(2,1)}, u32[]{:S(2)}) copy-start(bf16[1024,256]{1,0:T(8,128)(2,1)} %second_ref.1) | copy-start | bytes 1572868
  49.4 3.4 %copy-start.4 = (bf16[256,256]{1,0:T(8,128)(2,1)S(1)}, bf16[256,256]{1,0:T(8,128)(2,1)}, u32[]{:S(2)}) copy-start(bf16[256,256]{1,0:T(8,128)(2,1)} %exit_ref.5) | copy-start | bytes 393220
  103.3 14.6 %copy-start = (f32[48,16,256]{2,1,0:T(8,128)S(1)}, f32[48,16,256]{2,1,0:T(8,128)}, u32[]{:S(2)}) copy-start(f32[48,16,256]{2,1,0:T(8,128)} %param.15) | copy-start | bytes 2359300

commit v5 on v4

--- a/solution.py
+++ b/solution.py
@@ -15,7 +15,6 @@
 EPSILON = 1e-05
 LOG2E = 1.4426950408889634
 VMEM_LIMIT = 48 * 1024 * 1024
-WHOLE_VMEM = 63 * 1024 * 1024
 
 SEQ = ("z_low", "x")
 
@@ -40,44 +39,25 @@
     return (y * CORES + core) * Z_HIGH + z_high
 
 
-def centre_kernel(columns, *refs):
+def centre_kernel(columns, base_ref, out_ref):
+    values = base_ref[...]
+    centred = (values - jnp.mean(values, axis=-1, keepdims=True)).astype(jnp.bfloat16)
+    for block in range(base_ref.shape[0] // columns):
+        place = by_device(block) * columns
+        out_ref[place : place + columns] = centred[block * columns : (block + 1) * columns]
+
+
+def pack_kernel(*refs):
+    packed_ref = refs[-1]
+    channels = packed_ref.shape[1]
+    packed_ref[...] = jnp.zeros_like(packed_ref)
     places = (GAIN, SHIFT, ROW_GATE, ROW_EXIT, COL_GATE, COL_EXIT, SECOND, FIRST)
-    small = len(places)
-    base_hbm, small_hbm = refs[0], refs[1 : 1 + small]
-    out_ref, packed_ref, base_ref = refs[1 + small : 4 + small]
-    small_refs, (base_sem, small_sem) = refs[4 + small : 4 + 2 * small], refs[-2:]
-    rows, channels = base_ref.shape
-    parts = base_sem.shape[0]
-    part = rows // parts
-    assert part % (columns * Z_HIGH * CORES) == 0
-    copies = [
-        pltpu.make_async_copy(
-            base_hbm.at[pl.ds(i * part, part)], base_ref.at[pl.ds(i * part, part)], base_sem.at[i]
-        )
-        for i in range(parts)
-    ]
-    for copy in copies:
-        copy.start()
-    small_copies = [
-        pltpu.make_async_copy(small_hbm[i], small_refs[i], small_sem.at[i]) for i in range(small)
-    ]
-    for copy in small_copies:
-        copy.start()
-    for i in range(parts):
-        copies[i].wait()
-        values = base_ref[i * part : (i + 1) * part]
-        centred = (values - jnp.mean(values, axis=-1, keepdims=True)).astype(jnp.bfloat16)
-        for first in range(0, part, columns):
-            place = by_device((i * part + first) // columns) * columns
-            out_ref[place : place + columns] = centred[first : first + columns]
-    packed_ref[...] = jnp.zeros_like(packed_ref)
-    for i, place in enumerate(places):
-        small_copies[i].wait()
-        count, width = small_refs[i].shape
+    for place, ref in zip(places, refs):
+        count, width = ref.shape
         for j in range(count):
             for k in range(width // channels):
                 row = place + j + k
-                packed_ref[row : row + 1] = small_refs[i][j : j + 1, k * channels : (k + 1) * channels]
+                packed_ref[row : row + 1] = ref[j : j + 1, k * channels : (k + 1) * channels]
 
 
 def spans(rows, block):
@@ -101,25 +81,35 @@
 def attend(queries, gates, key_ref, value_ref):
     channels = queries.shape[1]
     head_size = channels // HEADS
+    per_tile = LANES // head_size
     lane_head = lax.broadcasted_iota(jnp.int32, (1, LANES), 1) // head_size
+
+    def score(number):
+        tile, head = divmod(number, per_tile)
+        lanes = slice(tile * LANES, (tile + 1) * LANES)
+        mask = (lane_head == head).astype(jnp.float32)
+        return lax.dot_general(
+            queries[:, lanes] * mask.astype(jnp.bfloat16),
+            key_ref[:, lanes],
+            (((1,), (1,)), ((), ())),
+            preferred_element_type=jnp.float32,
+        )
+
     gated = []
-    for tile in range(channels // LANES):
-        lanes = slice(tile * LANES, (tile + 1) * LANES)
-        keys = key_ref[:, lanes]
-        mixed = jnp.zeros((queries.shape[0], LANES), jnp.float32)
-        for head in range(LANES // head_size):
-            mask = (lane_head == head).astype(jnp.float32)
-            scores = lax.dot_general(
-                queries[:, lanes] * mask.astype(jnp.bfloat16),
-                keys,
-                (((1,), (1,)), ((), ())),
-                preferred_element_type=jnp.float32,
-            )
-            peak = jnp.max(scores, axis=-1, keepdims=True)
-            weights = jnp.exp2(scores - peak).astype(jnp.bfloat16)
-            result = matmul(weights, value_ref[tile])
-            mixed = jnp.where(lane_head == head, result[:, :LANES] / result[:, LANES:], mixed)
-        gated.append((gates[:, lanes] * mixed).astype(jnp.bfloat16))
+    following = score(0)
+    for number in range(HEADS):
+        scores = following
+        if number + 1 < HEADS:
+            following = score(number + 1)
+        tile, head = divmod(number, per_tile)
+        peak = jnp.max(scores, axis=-1, keepdims=True)
+        weights = jnp.exp2(scores - peak).astype(jnp.bfloat16)
+        result = matmul(weights, value_ref[tile])
+        ratio = result[:, :LANES] / result[:, LANES:]
+        mixed = ratio if head == 0 else jnp.where(lane_head == head, ratio, mixed)
+        if head + 1 == per_tile:
+            gates_here = gates[:, tile * LANES : (tile + 1) * LANES]
+            gated.append((gates_here * mixed).astype(jnp.bfloat16))
     return jnp.concatenate(gated, axis=1)
 
 
@@ -220,14 +210,12 @@
         out_ref[:, tile * LANES : (tile + 1) * LANES] = turned_ref[tile] + mean
 
 
-def call(
-    kernel, out_shape, scratch=(), flops=0, transcendentals=0, name=None, vmem=VMEM_LIMIT, **specs
-):
+def call(kernel, out_shape, scratch=(), flops=0, transcendentals=0, name=None, **specs):
     return pl.pallas_call(
         kernel,
         out_shape=out_shape,
         scratch_shapes=list(scratch),
-        compiler_params=pltpu.CompilerParams(vmem_limit_bytes=vmem),
+        compiler_params=pltpu.CompilerParams(vmem_limit_bytes=VMEM_LIMIT),
         cost_estimate=pl.CostEstimate(
             flops=flops, bytes_accessed=2**21, transcendentals=transcendentals
         ),
@@ -286,20 +274,11 @@
         feedforward_second_offset.reshape(1, -1),
         feedforward_first_offset.reshape(1, -1),
     ]
-    parts = max(rows // (2 * seq_count * Z_HIGH * CORES), 1)
     vmem = pl.BlockSpec(memory_space=pltpu.VMEM)
-    hbm = pl.BlockSpec(memory_space=pltpu.HBM)
-    centred, packed = call(
-        functools.partial(centre_kernel, seq_count),
-        (narrow, jax.ShapeDtypeStruct((PACKED, channels), jnp.float32)),
-        [pltpu.VMEM((rows, channels), jnp.float32)]
-        + [pltpu.VMEM(array.shape, jnp.float32) for array in small]
-        + [pltpu.SemaphoreType.DMA((count,)) for count in (parts, len(small))],
-        name="centre",
-        vmem=WHOLE_VMEM,
-        in_specs=[hbm] * (1 + len(small)),
-        out_specs=(vmem, vmem),
-    )(base, *small)
+    packed = call(
+        pack_kernel, jax.ShapeDtypeStruct((PACKED, channels), jnp.float32), name="pack"
+    )(*small, horizontal_entry_matrix, horizontal_exit_matrix)
+    centred = call(functools.partial(centre_kernel, seq_count), narrow, name="centre")(base)
     core = lax.axis_index("core").astype(jnp.int32).reshape(1)
     smem = pl.BlockSpec(memory_space=pltpu.SMEM)
     half = jax.ShapeDtypeStruct((rows // CORES, channels), jnp.bfloat16)

time: 119 us -> 119 us (level)
  local copies, waits for them, and re-layouts: 0.35 us -> 2.13 us
  Pallas kernels: 19.2 us -> 17.8 us
    unnamed x16 -> x32, local copies, waits for them, and re-layouts: 0.05 us -> 1.83 us
    pallas_call x1 -> x2, Pallas kernels: 2.29 us -> 0.93 us  [the longest x1 0.92 us: shards(): call(functools.partial(centre_kernel, seq_count), narrow, name='centre')]
where the time goes in v5:
time: 119 us
  blocking collectives  56.6 us (48%)
  starting transfers between devices  23.2 us (19%)
  waiting for transfers between devices  18.8 us (16%)
  Pallas kernels  17.8 us (15%)
  local copies, waits for them, and re-layouts  2.13 us (2%)
    all_to_all x2, blocking collectives, exchange(): lax.all_to_all(values.reshape(count, rows // count, channels), axes, spli...  56.6 us
    all_to_all x1, starting transfers between devices, exchange(): lax.all_to_all(values.reshape(count, rows // count, channels), axes, spli...  21.2 us
    all_to_all x1, waiting for transfers between devices, exchange(): lax.all_to_all(values.reshape(count, rows // count, channels), axes, spli...  18.8 us
    pallas_call x1, Pallas kernels, shards(): call(col_kernel, narrow, work, flops=attention_flops + 16 * rows * channe...  7.63 us
    pallas_call x1, Pallas kernels, shards(): call(functools.partial(row_send_kernel, seq_count), (half, *(jax.ShapeDty...  4.3 us
    pallas_call x1, Pallas kernels, shards(): call(functools.partial(row_keep_kernel, seq_count), half, flops=attention...  3.4 us
  transfers between devices with their start and end apart: 2, of which 1 were waited for; matrix products, arithmetic and copies ran while one was open for 0% of the time, Pallas kernels for 3%

profile of v5, /device:TPU:1, one launch (start us, length us, event | category | flops | bytes accessed | tf_op | source)
XLA Modules:
  0.0 118.8 jit_solution(13793817182717722630)
XLA Ops:
  0.0 1.1 copy-done
  1.1 0.9 centre.1
  2.1 0.0 copy-start.14
  2.1 21.2 %all-to-all-start = ((bf16[48,16,256]{2,1,0:T(8,128)(2,1)}), bf16[48,16,256]{2,1,0:T(8,128)(2,1)S(1)}, u32[]{:S(2)}, u32[]{:S(2)}) async-start(bf16[48,16,256]{2,1,0:T(8,128)(2,1)} %bitcast.2), calls=%async_computation | async-start | bytes 786432 | tf_op jit(solution)/shard_map/all_to_all | solution.py:230
  23.3 0.0 copy-start.10
  23.3 0.0 copy-start.9
  23.4 0.6 copy-done.10
  24.0 0.0 copy-done.9
  24.0 0.0 copy-done.8
  24.0 0.0 copy-done.11
  24.0 18.8 %all-to-all-done = bf16[48,16,256]{2,1,0:T(8,128)(2,1)S(1)} async-done(((bf16[48,16,256]{2,1,0:T(8,128)(2,1)}), bf16[48,16,256]{2,1,0:T(8,128)(2,1)S(1)}, u32[]{:S(2)}, u32[]{:S(2)}) %all-to-all-start) | async-done | bytes 393248 | tf_op jit(solution)/shard_map/all_to_all | solution.py:230
  42.8 4.3 %row_attention_send.1 = (bf16[384,256]{1,0:T(8,128)(2,1)S(1)}, bf16[768,256]{1,0:T(8,128)(2,1)S(1)}, bf16[768,256]{1,0:T(8,128)(2,1)S(1)}, bf16[2,768,256]{2,1,0:T(8,128)(2,1)S(1)}, f32[768,256]{1,0:T(8,128)S(1)}) custom-call(s32[1]{0:T(128)} %bitcast.1.core_ref, bf16[768,256]{1,0:T(8,128)(2,1)S(1)} %bitcast.16, bf16[256,1024]{1,0:T(8,128)(2,1)S(1)} %copy-done.2, ...), custom_call_target="tpu_custom_call" | custom-call | flops 553648128 | bytes 2097152 | tf_op jit(solution)/shard_map/row_attention_send/pallas_call | solution.py:286
  47.1 2.0 %collective-permute-start = (bf16[384,256]{1,0:T(8,128)(2,1)S(1)}, bf16[384,256]{1,0:T(8,128)(2,1)S(1)}, u32[]{:S(2)}, u32[]{:S(2)}) collective-permute-start(bf16[384,256]{1,0:T(8,128)(2,1)S(1)} %get-tuple-element.14), channel_id=1, source_target_pairs={{0,1},{1,0},{2,3},{3,2},{4,5},{5,4},{6,7},{7,6},{8,9},{9,8},{10,11... | collective-permute-start | bytes 589832 | tf_op jit(solution)/shard_map/ppermute | solution.py:295
  49.2 0.0 copy-start.5
  49.2 0.0 copy-start.7
  49.2 3.4 %row_attention_keep.1.kept_ref = bf16[384,256]{1,0:T(8,128)(2,1)S(1)} custom-call(s32[1]{0:T(128)} %bitcast.1.core_ref, bf16[768,256]{1,0:T(8,128)(2,1)S(1)} %bitcast.17, bf16[256,256]{1,0:T(8,128)(2,1)S(1)} %copy-done.6, f32[16,256]{1,0:T(8,128)S(1)} %pack.1.packed_ref, bf16[768,256]{1,0:T(8,128)(2,1)S(1)} %get-tuple-element.10.refs_0_, ...), custom_call_target="tpu_custom_call" | custom-call | flops 553648128 | bytes 2097152 | tf_op jit(solution)/shard_map/row_attention_keep/pallas_call | solution.py:296
  52.7 0.3 turn.1
  53.0 0.2 reshape.55
  53.1 42.1 %all_to_all.15 = bf16[384,2,256]{2,1,0:T(2,128)(2,1)S(1)} all-to-all(bf16[384,2,256]{2,1,0:T(2,128)(2,1)S(1)} %reshape.55), channel_id=1, replica_groups=mesh['z_low'=4,'x'=4,'z_high'=3,'y'=8,'core'=2] {'z_low','x','y','z_high'}, dimensions={0} | all-to-all | bytes 786432 | tf_op jit(solution)/shard_map/all_to_all | solution.py:230
  95.2 0.2 reshape.56.residual_ref
  95.4 7.6 %col_attention_transition.1 = bf16[768,256]{1,0:T(8,128)(2,1)S(1)} custom-call(bf16[768,256]{1,0:T(8,128)(2,1)S(1)} %reshape.56.residual_ref, bf16[256,1024]{1,0:T(8,128)(2,1)S(1)} %copy-done.3, bf16[256,256]{1,0:T(8,128)(2,1)S(1)} %copy-done.7, bf16[256,1024]{1,0:T(8,128)(2,1)S(1)} %copy-done.4, bf16[1024,256]{1,0:T(8,128)(2,1)S(1)} %copy-done.5, ...), custom_call_target="tpu_custom_call" | custom-call | flops 1912602624 | bytes 2097152 | tf_op jit(solution)/shard_map/col_attention_transition/pallas_call | solution.py:319
  103.0 0.0 copy-start.1
  103.0 14.6 %all_to_all.16 = bf16[16,48,256]{2,1,0:T(8,128)(2,1)S(1)} all-to-all(bf16[16,48,256]{2,1,0:T(8,128)(2,1)S(1)} %bitcast.18), channel_id=1, replica_groups=mesh['z_low'=4,'x'=4,'z_high'=3,'y'=8,'core'=2] {'z_low','x'}, dimensions={0} | all-to-all | bytes 786432 | tf_op jit(solution)/shard_map/all_to_all | solution.py:230
  117.6 1.2 %home.1 = f32[768,256]{1,0:T(8,128)} custom-call(f32[768,256]{1,0:T(8,128)S(1)} %bitcast.14, bf16[768,256]{1,0:T(8,128)(2,1)S(1)} %bitcast.15), custom_call_target="tpu_custom_call" | custom-call | bytes 2097152 | tf_op jit(solution)/shard_map/home/pallas_call | solution.py:331
  (23 shorter events, 0.1 us)
Async XLA Ops:
  0.0 1.1 copy-start
  2.1 21.3 %copy-start.2 = (bf16[256,1024]{1,0:T(8,128)(2,1)S(1)}, bf16[256,1024]{1,0:T(8,128)(2,1)}, u32[]{:S(2)}) copy-start(bf16[256,1024]{1,0:T(8,128)(2,1)} %entry_ref.2) | copy-start | bytes 1572868
  2.1 21.3 %copy-start.6 = (bf16[256,256]{1,0:T(8,128)(2,1)S(1)}, bf16[256,256]{1,0:T(8,128)(2,1)}, u32[]{:S(2)}) copy-start(bf16[256,256]{1,0:T(8,128)(2,1)} %exit_ref.4) | copy-start | bytes 393220
  2.1 21.3 %copy-start.12 = (f32[256]{0:T(256)S(1)}, f32[256]{0:T(256)}, u32[]{:S(2)}) copy-start(f32[256]{0:T(256)} %param.21) | copy-start | bytes 3076
  2.1 21.3 %copy-start.13 = (f32[256]{0:T(256)S(1)}, f32[256]{0:T(256)}, u32[]{:S(2)}) copy-start(f32[256]{0:T(256)} %param.23) | copy-start | bytes 3076
  2.1 21.3 %copy-start.14 = (f32[256]{0:T(256)S(1)}, f32[256]{0:T(256)}, u32[]{:S(2)}) copy-start(f32[256]{0:T(256)} %param.25) | copy-start | bytes 3076
  2.1 21.3 %copy-start.15 = (f32[256]{0:T(256)S(1)}, f32[256]{0:T(256)}, u32[]{:S(2)}) copy-start(f32[256]{0:T(256)} %param.29) | copy-start | bytes 3076
  2.1 40.7 %all-to-all-start = ((bf16[48,16,256]{2,1,0:T(8,128)(2,1)}), bf16[48,16,256]{2,1,0:T(8,128)(2,1)S(1)}, u32[]{:S(2)}, u32[]{:S(2)}) async-start(bf16[48,16,256]{2,1,0:T(8,128)(2,1)} %bitcast.2), calls=%async_computation | async-start | bytes 786432 | tf_op jit(solution)/shard_map/all_to_all | solution.py:230
  23.3 0.7 copy-start.10
  23.3 0.7 copy-start.9
  23.3 0.7 copy-start.8
  23.3 0.7 copy-start.11
  47.1 5.5 %collective-permute-start = (bf16[384,256]{1,0:T(8,128)(2,1)S(1)}, bf16[384,256]{1,0:T(8,128)(2,1)S(1)}, u32[]{:S(2)}, u32[]{:S(2)}) collective-permute-start(bf16[384,256]{1,0:T(8,128)(2,1)S(1)} %get-tuple-element.14), channel_id=1, source_target_pairs={{0,1},{1,0},{2,3},{3,2},{4,5},{5,4},{6,7},{7,6},{8,9},{9,8},{10,11... | collective-permute-start | bytes 589832 | tf_op jit(solution)/shard_map/ppermute | solution.py:295
  49.2 3.5 %copy-start.3 = (bf16[256,1024]{1,0:T(8,128)(2,1)S(1)}, bf16[256,1024]{1,0:T(8,128)(2,1)}, u32[]{:S(2)}) copy-start(bf16[256,1024]{1,0:T(8,128)(2,1)} %entry_ref.3) | copy-start | bytes 1572868
  49.2 3.5 %copy-start.4 = (bf16[256,1024]{1,0:T(8,128)(2,1)S(1)}, bf16[256,1024]{1,0:T(8,128)(2,1)}, u32[]{:S(2)}) copy-start(bf16[256,1024]{1,0:T(8,128)(2,1)} %first_ref.1) | copy-start | bytes 1572868
  49.2 3.5 %copy-start.5 = (bf16[1024,256]{1,0:T(8,128)(2,1)S(1)}, bf16[1024,256]{1,0:T(8,128)(2,1)}, u32[]{:S(2)}) copy-start(bf16[1024,256]{1,0:T(8,128)(2,1)} %second_ref.1) | copy-start | bytes 1572868
  49.2 3.5 %copy-start.7 = (bf16[256,256]{1,0:T(8,128)(2,1)S(1)}, bf16[256,256]{1,0:T(8,128)(2,1)}, u32[]{:S(2)}) copy-start(bf16[256,256]{1,0:T(8,128)(2,1)} %exit_ref.5) | copy-start | bytes 393220
  103.0 14.6 %copy-start.1 = (f32[48,16,256]{2,1,0:T(8,128)S(1)}, f32[48,16,256]{2,1,0:T(8,128)}, u32[]{:S(2)}) copy-start(f32[48,16,256]{2,1,0:T(8,128)} %param.15) | copy-start | bytes 2359300

commit v6 on v5

--- a/solution.py
+++ b/solution.py
@@ -78,7 +78,7 @@
         gate_ref[span, :] = jax.nn.sigmoid(matmul(normed, entry_ref[:, 3 * channels :]) + gate)
 
 
-def attend(queries, gates, key_ref, value_ref):
+def attend(queries, gates, key_ref, value_ref, early=False):
     channels = queries.shape[1]
     head_size = channels // HEADS
     per_tile = LANES // head_size
@@ -96,10 +96,10 @@
         )
 
     gated = []
-    following = score(0)
+    following = score(0) if early else None
     for number in range(HEADS):
-        scores = following
-        if number + 1 < HEADS:
+        scores = following if early else score(number)
+        if early and number + 1 < HEADS:
             following = score(number + 1)
         tile, head = divmod(number, per_tile)
         peak = jnp.max(scores, axis=-1, keepdims=True)
@@ -182,7 +182,7 @@
     for span in spans(rows, QUERY_ROWS):
         after = residual_ref[span, :].astype(jnp.float32) + (
             matmul(
-                attend(query_ref[span, :], gate_ref[span, :], key_ref, value_ref), exit_ref[...]
+                attend(query_ref[span, :], gate_ref[span, :], key_ref, value_ref, True), exit_ref[...]
             ) + packed_ref[COL_EXIT : COL_EXIT + 1]
         )
         normed = normalize(after, packed_ref[GAIN + 2 : GAIN + 3], packed_ref[SHIFT + 2 : SHIFT + 3])
@@ -196,7 +196,7 @@
         out_ref[span, :] = (after + update).astype(jnp.bfloat16)
 
 
-def home_kernel(residues, base_ref, values_ref, out_ref, turned_ref):
+def home_kernel(residues, base_ref, values_ref, out_hbm, turned_ref, out_ref, sem):
     rows = base_ref.shape[0]
     seqs = rows // residues
     for tile in range(turned_ref.shape[0]):
@@ -205,9 +205,22 @@
             turned_ref.at[tile][pl.ds(item, seqs, stride=residues), :] = values_ref[
                 item * seqs : (item + 1) * seqs, lanes
             ].astype(jnp.float32)
-    mean = jnp.mean(base_ref[...], axis=-1, keepdims=True)
-    for tile in range(turned_ref.shape[0]):
-        out_ref[:, tile * LANES : (tile + 1) * LANES] = turned_ref[tile] + mean
+    parts = sem.shape[0]
+    part = rows // parts
+    copies = []
+    for i in range(parts):
+        span = slice(i * part, (i + 1) * part)
+        mean = jnp.mean(base_ref[span, :], axis=-1, keepdims=True)
+        for tile in range(turned_ref.shape[0]):
+            lanes = slice(tile * LANES, (tile + 1) * LANES)
+            out_ref[span, lanes] = turned_ref[tile, span, :] + mean
+        copy = pltpu.make_async_copy(
+            out_ref.at[pl.ds(i * part, part)], out_hbm.at[pl.ds(i * part, part)], sem.at[i]
+        )
+        copy.start()
+        copies.append(copy)
+    for copy in copies:
+        copy.wait()
 
 
 def call(kernel, out_shape, scratch=(), flops=0, transcendentals=0, name=None, **specs):
@@ -328,9 +341,14 @@
         *col_weights,
         packed,
     )
-    home = call(functools.partial(home_kernel, res_local), wide, [split], name="home")(
-        base, exchange(updated, SEQ)
-    )
+    home = call(
+        functools.partial(home_kernel, res_local),
+        wide,
+        [split, pltpu.VMEM((rows, channels), jnp.float32), pltpu.SemaphoreType.DMA((3,))],
+        name="home",
+        in_specs=[vmem, vmem],
+        out_specs=pl.BlockSpec(memory_space=pl.ANY),
+    )(base, exchange(updated, SEQ))
     return home.reshape(seq_local, res_local, channels)
 
 

time: 119 us -> 119 us (level)
  no operation moved by 1% of the time
where the time goes in v6:
time: 119 us
  blocking collectives  56.6 us (48%)
  starting transfers between devices  23.2 us (19%)
  waiting for transfers between devices  18.8 us (16%)
  Pallas kernels  17.8 us (15%)
  local copies, waits for them, and re-layouts  2.13 us (2%)
    all_to_all x2, blocking collectives, exchange(): lax.all_to_all(values.reshape(count, rows // count, channels), axes, spli...  56.6 us
    all_to_all x1, starting transfers between devices, exchange(): lax.all_to_all(values.reshape(count, rows // count, channels), axes, spli...  21.2 us
    all_to_all x1, waiting for transfers between devices, exchange(): lax.all_to_all(values.reshape(count, rows // count, channels), axes, spli...  18.8 us
    pallas_call x1, Pallas kernels, shards(): call(col_kernel, narrow, work, flops=attention_flops + 16 * rows * channe...  7.63 us
    pallas_call x1, Pallas kernels, shards(): call(functools.partial(row_send_kernel, seq_count), (half, *(jax.ShapeDty...  4.37 us
    pallas_call x1, Pallas kernels, shards(): call(functools.partial(row_keep_kernel, seq_count), half, flops=attention...  3.44 us
  transfers between devices with their start and end apart: 2, of which 1 were waited for; matrix products, arithmetic and copies ran while one was open for 0% of the time, Pallas kernels for 3%

profile of v6, /device:TPU:1, one launch (start us, length us, event | category | flops | bytes accessed | tf_op | source)
XLA Modules:
  0.0 119.0 jit_solution(6130634420805809233)
XLA Ops:
  0.0 1.1 copy-done
  1.1 0.9 centre.1
  2.1 0.0 copy-start.14
  2.1 0.0 copy-start.15
  2.1 21.2 %all-to-all-start = ((bf16[48,16,256]{2,1,0:T(8,128)(2,1)}), bf16[48,16,256]{2,1,0:T(8,128)(2,1)S(1)}, u32[]{:S(2)}, u32[]{:S(2)}) async-start(bf16[48,16,256]{2,1,0:T(8,128)(2,1)} %bitcast.2), calls=%async_computation | async-start | bytes 786432 | tf_op jit(solution)/shard_map/all_to_all | solution.py:243
  23.3 0.0 copy-start.8
  23.3 0.0 copy-start.11
  23.4 0.6 copy-done.10
  24.0 0.0 copy-done.9
  24.0 0.0 copy-done.8
  24.0 0.0 copy-done.11
  24.0 18.8 %all-to-all-done = bf16[48,16,256]{2,1,0:T(8,128)(2,1)S(1)} async-done(((bf16[48,16,256]{2,1,0:T(8,128)(2,1)}), bf16[48,16,256]{2,1,0:T(8,128)(2,1)S(1)}, u32[]{:S(2)}, u32[]{:S(2)}) %all-to-all-start) | async-done | bytes 393248 | tf_op jit(solution)/shard_map/all_to_all | solution.py:243
  42.8 4.4 %row_attention_send.1 = (bf16[384,256]{1,0:T(8,128)(2,1)S(1)}, bf16[768,256]{1,0:T(8,128)(2,1)S(1)}, bf16[768,256]{1,0:T(8,128)(2,1)S(1)}, bf16[2,768,256]{2,1,0:T(8,128)(2,1)S(1)}, f32[768,256]{1,0:T(8,128)S(1)}) custom-call(s32[1]{0:T(128)} %bitcast.1.core_ref, bf16[768,256]{1,0:T(8,128)(2,1)S(1)} %bitcast.16, bf16[256,1024]{1,0:T(8,128)(2,1)S(1)} %copy-done.2, ...), custom_call_target="tpu_custom_call" | custom-call | flops 553648128 | bytes 2097152 | tf_op jit(solution)/shard_map/row_attention_send/pallas_call | solution.py:299
  47.2 2.0 %collective-permute-start = (bf16[384,256]{1,0:T(8,128)(2,1)S(1)}, bf16[384,256]{1,0:T(8,128)(2,1)S(1)}, u32[]{:S(2)}, u32[]{:S(2)}) collective-permute-start(bf16[384,256]{1,0:T(8,128)(2,1)S(1)} %get-tuple-element.14), channel_id=1, source_target_pairs={{0,1},{1,0},{2,3},{3,2},{4,5},{5,4},{6,7},{7,6},{8,9},{9,8},{10,11... | collective-permute-start | bytes 589832 | tf_op jit(solution)/shard_map/ppermute | solution.py:308
  49.2 0.0 copy-start.3
  49.2 0.0 copy-start.4
  49.3 3.4 %row_attention_keep.1.kept_ref = bf16[384,256]{1,0:T(8,128)(2,1)S(1)} custom-call(s32[1]{0:T(128)} %bitcast.1.core_ref, bf16[768,256]{1,0:T(8,128)(2,1)S(1)} %bitcast.17, bf16[256,256]{1,0:T(8,128)(2,1)S(1)} %copy-done.6, f32[16,256]{1,0:T(8,128)S(1)} %pack.1.packed_ref, bf16[768,256]{1,0:T(8,128)(2,1)S(1)} %get-tuple-element.10.refs_0_, ...), custom_call_target="tpu_custom_call" | custom-call | flops 553648128 | bytes 2097152 | tf_op jit(solution)/shard_map/row_attention_keep/pallas_call | solution.py:309
  52.8 0.3 turn.1
  53.1 0.2 reshape.55
  53.2 42.1 %all_to_all.15 = bf16[384,2,256]{2,1,0:T(2,128)(2,1)S(1)} all-to-all(bf16[384,2,256]{2,1,0:T(2,128)(2,1)S(1)} %reshape.55), channel_id=1, replica_groups=mesh['z_low'=4,'x'=4,'z_high'=3,'y'=8,'core'=2] {'z_low','x','y','z_high'}, dimensions={0} | all-to-all | bytes 786432 | tf_op jit(solution)/shard_map/all_to_all | solution.py:243
  95.3 0.2 reshape.56.residual_ref
  95.5 7.6 %col_attention_transition.1 = bf16[768,256]{1,0:T(8,128)(2,1)S(1)} custom-call(bf16[768,256]{1,0:T(8,128)(2,1)S(1)} %reshape.56.residual_ref, bf16[256,1024]{1,0:T(8,128)(2,1)S(1)} %copy-done.3, bf16[256,256]{1,0:T(8,128)(2,1)S(1)} %copy-done.7, bf16[256,1024]{1,0:T(8,128)(2,1)S(1)} %copy-done.4, bf16[1024,256]{1,0:T(8,128)(2,1)S(1)} %copy-done.5, ...), custom_call_target="tpu_custom_call" | custom-call | flops 1912602624 | bytes 2097152 | tf_op jit(solution)/shard_map/col_attention_transition/pallas_call | solution.py:332
  103.1 14.6 %all_to_all.16 = bf16[16,48,256]{2,1,0:T(8,128)(2,1)S(1)} all-to-all(bf16[16,48,256]{2,1,0:T(8,128)(2,1)S(1)} %bitcast.18), channel_id=1, replica_groups=mesh['z_low'=4,'x'=4,'z_high'=3,'y'=8,'core'=2] {'z_low','x'}, dimensions={0} | all-to-all | bytes 786432 | tf_op jit(solution)/shard_map/all_to_all | solution.py:243
  117.7 1.2 home.1
  (23 shorter events, 0.1 us)
Async XLA Ops:
  0.0 1.1 copy-start
  2.1 21.3 %copy-start.2 = (bf16[256,1024]{1,0:T(8,128)(2,1)S(1)}, bf16[256,1024]{1,0:T(8,128)(2,1)}, u32[]{:S(2)}) copy-start(bf16[256,1024]{1,0:T(8,128)(2,1)} %entry_ref.2) | copy-start | bytes 1572868
  2.1 21.3 %copy-start.6 = (bf16[256,256]{1,0:T(8,128)(2,1)S(1)}, bf16[256,256]{1,0:T(8,128)(2,1)}, u32[]{:S(2)}) copy-start(bf16[256,256]{1,0:T(8,128)(2,1)} %exit_ref.4) | copy-start | bytes 393220
  2.1 21.3 %copy-start.12 = (f32[256]{0:T(256)S(1)}, f32[256]{0:T(256)}, u32[]{:S(2)}) copy-start(f32[256]{0:T(256)} %param.21) | copy-start | bytes 3076
  2.1 21.3 %copy-start.13 = (f32[256]{0:T(256)S(1)}, f32[256]{0:T(256)}, u32[]{:S(2)}) copy-start(f32[256]{0:T(256)} %param.23) | copy-start | bytes 3076
  2.1 21.3 %copy-start.14 = (f32[256]{0:T(256)S(1)}, f32[256]{0:T(256)}, u32[]{:S(2)}) copy-start(f32[256]{0:T(256)} %param.25) | copy-start | bytes 3076
  2.1 21.3 %copy-start.15 = (f32[256]{0:T(256)S(1)}, f32[256]{0:T(256)}, u32[]{:S(2)}) copy-start(f32[256]{0:T(256)} %param.29) | copy-start | bytes 3076
  2.1 40.7 %all-to-all-start = ((bf16[48,16,256]{2,1,0:T(8,128)(2,1)}), bf16[48,16,256]{2,1,0:T(8,128)(2,1)S(1)}, u32[]{:S(2)}, u32[]{:S(2)}) async-start(bf16[48,16,256]{2,1,0:T(8,128)(2,1)} %bitcast.2), calls=%async_computation | async-start | bytes 786432 | tf_op jit(solution)/shard_map/all_to_all | solution.py:243
  23.3 0.7 copy-start.10
  23.3 0.7 copy-start.9
  23.3 0.7 copy-start.8
  23.3 0.7 copy-start.11
  47.2 5.5 %collective-permute-start = (bf16[384,256]{1,0:T(8,128)(2,1)S(1)}, bf16[384,256]{1,0:T(8,128)(2,1)S(1)}, u32[]{:S(2)}, u32[]{:S(2)}) collective-permute-start(bf16[384,256]{1,0:T(8,128)(2,1)S(1)} %get-tuple-element.14), channel_id=1, source_target_pairs={{0,1},{1,0},{2,3},{3,2},{4,5},{5,4},{6,7},{7,6},{8,9},{9,8},{10,11... | collective-permute-start | bytes 589832 | tf_op jit(solution)/shard_map/ppermute | solution.py:308
  49.2 3.5 %copy-start.3 = (bf16[256,1024]{1,0:T(8,128)(2,1)S(1)}, bf16[256,1024]{1,0:T(8,128)(2,1)}, u32[]{:S(2)}) copy-start(bf16[256,1024]{1,0:T(8,128)(2,1)} %entry_ref.3) | copy-start | bytes 1572868
  49.2 3.5 %copy-start.4 = (bf16[256,1024]{1,0:T(8,128)(2,1)S(1)}, bf16[256,1024]{1,0:T(8,128)(2,1)}, u32[]{:S(2)}) copy-start(bf16[256,1024]{1,0:T(8,128)(2,1)} %first_ref.1) | copy-start | bytes 1572868
  49.2 3.5 %copy-start.5 = (bf16[1024,256]{1,0:T(8,128)(2,1)S(1)}, bf16[1024,256]{1,0:T(8,128)(2,1)}, u32[]{:S(2)}) copy-start(bf16[1024,256]{1,0:T(8,128)(2,1)} %second_ref.1) | copy-start | bytes 1572868
  49.3 3.5 %copy-start.7 = (bf16[256,256]{1,0:T(8,128)(2,1)S(1)}, bf16[256,256]{1,0:T(8,128)(2,1)}, u32[]{:S(2)}) copy-start(bf16[256,256]{1,0:T(8,128)(2,1)} %exit_ref.5) | copy-start | bytes 393220
  103.1 14.6 %copy-start.1 = (f32[48,16,256]{2,1,0:T(8,128)S(1)}, f32[48,16,256]{2,1,0:T(8,128)}, u32[]{:S(2)}) copy-start(f32[48,16,256]{2,1,0:T(8,128)} %param.15) | copy-start | bytes 2359300
